TPU v7x, 32 devices: a whole 2x2x4 slice. The times are simulated.
32 devices in a mesh: gene: 8 (over y, x, core), cell: 4 (over z).
Axes of the slice: x: 2, y: 2, z: 4, core: 2. Of those that a mesh axis runs over, the one named last changes fastest.
Arguments:
- counts: int32 [8192, 20000], P('cell', 'gene'), may hold values from 0 to 16, as said below
- labels: int32 [8192], P(('cell', 'gene')), may hold values from 0 to 127
- noise_draw: float32 [8192, 10], P(('cell', 'gene')), may hold values from -6 to 6
- enc_weight: float32 [20000, 128], P('gene'), may hold values from -0.0390625 to 0.0390625
- enc_first: float32 [20000, 128], P('gene'), may hold values from -0.00015258789 to 0.00015258789
- enc_second: float32 [20000, 128], P('gene'), may hold values from 8.053339e-12 to 3.2213357e-11
- out_weight: float32 [2, 128, 20000], P(None, None, 'gene'), may hold values from -0.5 to 0.5
- out_first: float32 [2, 128, 20000], P(None, None, 'gene'), may hold values from -0.00015258789 to 0.00015258789
- out_second: float32 [2, 128, 20000], P(None, None, 'gene'), may hold values from 8.053339e-12 to 3.2213357e-11
- gene_param: float32 [3, 20000], P(None, 'gene'), may hold values from -1 to 1
- gene_first: float32 [3, 20000], P(None, 'gene'), may hold values from -0.00015258789 to 0.00015258789
- gene_second: float32 [3, 20000], P(None, 'gene'), may hold values from 8.053339e-12 to 3.2213357e-11
- head_weight: float32 [128, 20], replicated, may hold values from -0.5 to 0.5
- head_first: float32 [128, 20], replicated, may hold values from -0.00015258789 to 0.00015258789
- head_second: float32 [128, 20], replicated, may hold values from 8.053339e-12 to 3.2213357e-11
- head_bias: float32 [20], replicated, may hold values from -4 to 4
- bias_first: float32 [20], replicated, may hold values from -0.00015258789 to 0.00015258789
- bias_second: float32 [20], replicated, may hold values from 8.053339e-12 to 3.2213357e-11
- dec_weight: float32 [138, 128], replicated, may hold values from -0.5 to 0.5
- dec_first: float32 [138, 128], replicated, may hold values from -0.00015258789 to 0.00015258789
- dec_second: float32 [138, 128], replicated, may hold values from 8.053339e-12 to 3.2213357e-11
- norm_param: float32 [4, 128], replicated, may hold values from 0.5 to 1.5
- norm_first: float32 [4, 128], replicated, may hold values from -0.00015258789 to 0.00015258789
- norm_second: float32 [4, 128], replicated, may hold values from 8.053339e-12 to 3.2213357e-11
Outputs:
- loss_sum: float32 [], replicated
- grad_norm: float32 [], replicated
- enc_master: float32 [20000, 128], P('gene')
- enc_first_new: float32 [20000, 128], P('gene')
- enc_second_new: float32 [20000, 128], P('gene')
- out_master: float32 [2, 128, 20000], P(None, None, 'gene')
- out_first_new: float32 [2, 128, 20000], P(None, None, 'gene')
- out_second_new: float32 [2, 128, 20000], P(None, None, 'gene')
- gene_master: float32 [3, 20000], P(None, 'gene')
- gene_first_new: float32 [3, 20000], P(None, 'gene')
- gene_second_new: float32 [3, 20000], P(None, 'gene')
- head_master: float32 [128, 20], replicated
- head_first_new: float32 [128, 20], replicated
- head_second_new: float32 [128, 20], replicated
- bias_master: float32 [20], replicated
- bias_first_new: float32 [20], replicated
- bias_second_new: float32 [20], replicated
- dec_master: float32 [138, 128], replicated
- dec_first_new: float32 [138, 128], replicated
- dec_second_new: float32 [138, 128], replicated
- norm_master: float32 [4, 128], replicated
- norm_first_new: float32 [4, 128], replicated
- norm_second_new: float32 [4, 128], replicated
- enc_copy: bfloat16 [20000, 128], P('gene')
- out_copy: bfloat16 [2, 128, 20000], P(None, None, 'gene')
- head_copy: bfloat16 [128, 20], replicated
- dec_copy: bfloat16 [138, 128], replicated
Inputs may be any that keep to these rules, and one draw needn't show every extreme that they name: `counts`: every cell has a count of 1 or more in some gene.
All inputs are finite; a program needn't handle non-finite values.
Results may differ from a plain program's by a relative error of at most 0.0095.
Values may be sent and summed in bfloat16 or wider, within the bound.
No kernel may reach another device: no remote copies, remote signals or barrier semaphores. Data moves between devices by JAX's collectives and lax.ppermute only.
A program may use at most 256 MiB of HBM per device.

v0:
```python
import jax
import jax.numpy as jnp
from jax import lax
from jax.sharding import PartitionSpec as P

H = 128
L = 10
G = 20000
NB = 128
STEP = 10


HIGHEST = lax.Precision.HIGHEST
BETA_ONE = 0.9
BETA_TWO = 0.999
ADAM_EPS = 1e-08
DECAY_RATE = 0.01
CLIP_NORM = 0.25
NORM_EPS = 0.001


def merged_2(value, axis, combine):
    everything = jax.tree.map(lambda part: lax.all_gather(part, axis), value)
    first = jax.tree.map(lambda part: part[0], everything)

    def hop(k, so_far):
        return combine(so_far, jax.tree.map(lambda part: part[k], everything))

    return lax.fori_loop(1, lax.axis_size(axis), hop, first)


def sigmoid_unit(value):
    return value * jax.nn.sigmoid(value)


def unit_slope(value):
    sigma = jax.nn.sigmoid(value)
    return sigma * (1.0 + value * (1.0 - sigma))


def moments_sum(first_part, second_part):
    return lax.psum((first_part, second_part), ("gene", "cell"))


def norm_forward(hidden, gain, shift, total_cells):
    sum_one, sum_two = moments_sum(jnp.sum(hidden, 0), jnp.sum(hidden * hidden, 0))
    average = sum_one / total_cells
    inv_std = lax.rsqrt(sum_two / total_cells - average * average + NORM_EPS)
    normed = (hidden - average) * inv_std
    return (normed, inv_std, normed * gain + shift)


def norm_backward(upstream, normed, inv_std, gain, total_cells):
    shift_grad, gain_grad = moments_sum(jnp.sum(upstream, 0), jnp.sum(upstream * normed, 0))
    inner = upstream - shift_grad / total_cells - normed * gain_grad / total_cells
    return (gain * inv_std * inner, gain_grad, shift_grad)


def zinb_terms(counts, log_mean, dropout, log_theta):
    theta = jnp.exp(log_theta)
    log_both = jnp.logaddexp(log_theta, log_mean)
    soft_neg = jax.nn.softplus(-dropout)
    shifted = -dropout + theta * (log_theta - log_both)
    zero_case = jax.nn.softplus(shifted) - soft_neg
    fcounts = counts.astype(jnp.float32)
    theta_full = jnp.broadcast_to(theta, fcounts.shape)
    other_case = (
        -soft_neg
        + shifted
        + fcounts * (log_mean - log_both)
        + lax.lgamma(fcounts + theta_full)
        - lax.lgamma(theta_full)
        - lax.lgamma(fcounts + 1.0)
    )
    return jnp.where(counts == 0, zero_case, other_case)


def combine_parts(left, right):
    highest = jnp.maximum(left[0], right[0])
    merged = left[1] * jnp.exp(left[0] - highest) + right[1] * jnp.exp(right[0] - highest)
    return (highest, merged, left[2] + right[2])


def adam_update(master, first, second, grad, rate):
    first_new = BETA_ONE * first + (1.0 - BETA_ONE) * grad
    second_new = BETA_TWO * second + (1.0 - BETA_TWO) * grad * grad
    first_hat = first_new / (1.0 - BETA_ONE**STEP)
    second_hat = second_new / (1.0 - BETA_TWO**STEP)
    master_new = master - rate * (
        first_hat / (jnp.sqrt(second_hat) + ADAM_EPS) + DECAY_RATE * master
    )
    return (master_new, first_new, second_new)


def squared(value):
    return jnp.sum(value * value)


def per_device(
    counts,
    labels,
    noise_draw,
    enc_weight,
    enc_first,
    enc_second,
    out_weight,
    out_first,
    out_second,
    gene_param,
    gene_first,
    gene_second,
    head_weight,
    head_first,
    head_second,
    head_bias,
    bias_first,
    bias_second,
    dec_weight,
    dec_first,
    dec_second,
    norm_param,
    norm_first,
    norm_second,
):
    gene_devs = lax.axis_size("gene")
    cell_devs = lax.axis_size("cell")
    cells_here = noise_draw.shape[0]
    width = enc_weight.shape[1]
    total_cells = cells_here * gene_devs * cell_devs
    fcounts = counts.astype(jnp.float32)
    log_counts = jnp.log1p(fcounts).astype(jnp.bfloat16)
    enc_low = enc_weight.astype(jnp.bfloat16)
    partial_sums = jnp.dot(log_counts, enc_low, preferred_element_type=jnp.float32)
    arrived = lax.all_to_all(
        partial_sums.reshape(gene_devs, cells_here, width),
        "gene",
        split_axis=0,
        concat_axis=0,
        tiled=True,
    )
    enc_hidden = jnp.sum(arrived, axis=0)
    normed_one, inv_one, act_one = norm_forward(
        enc_hidden, norm_param[0], norm_param[1], total_cells
    )
    enc_out = sigmoid_unit(act_one).astype(jnp.bfloat16)
    head_low = head_weight.astype(jnp.bfloat16)
    head_out = jnp.dot(enc_out, head_low, preferred_element_type=jnp.float32) + head_bias
    latent_mean = head_out[:, :L]
    log_var = head_out[:, L:]
    spread = jnp.exp(0.5 * log_var)
    latent = latent_mean + spread * noise_draw
    kl_sum = 0.5 * jnp.sum(latent_mean * latent_mean + jnp.exp(log_var) - log_var - 1.0)
    onehot = (labels[:, None] == jnp.arange(NB)[None, :]).astype(jnp.bfloat16)
    dec_in = jnp.concatenate([latent.astype(jnp.bfloat16), onehot], 1)
    dec_low = dec_weight.astype(jnp.bfloat16)
    pre_two = jnp.dot(dec_in, dec_low, preferred_element_type=jnp.float32)
    normed_two, inv_two, act_two = norm_forward(pre_two, norm_param[2], norm_param[3], total_cells)
    dec_hidden = sigmoid_unit(act_two).astype(jnp.bfloat16)
    gathered = lax.all_gather(dec_hidden, "gene", axis=0, tiled=True)
    out_low = out_weight.astype(jnp.bfloat16)
    logits = jnp.dot(gathered, out_low[0], preferred_element_type=jnp.float32) + gene_param[0]
    dropout = jnp.dot(gathered, out_low[1], preferred_element_type=jnp.float32) + gene_param[1]
    local_top = jnp.max(logits, 1)
    local_exp = jnp.sum(jnp.exp(logits - local_top[:, None]), 1)
    highest, exp_sum, totals = merged_2(
        (local_top, local_exp, jnp.sum(fcounts, 1)), "gene", combine_parts
    )
    log_scale = logits - (highest + jnp.log(exp_sum))[:, None]
    log_total = jnp.log(totals)[:, None]

    def local_loss(scale_part, drop_part, theta_part):
        return -jnp.sum(zinb_terms(counts, log_total + scale_part, drop_part, theta_part))

    recon_sum, pull_back = jax.vjp(local_loss, log_scale, dropout, gene_param[2])
    grad_scale, grad_drop, grad_theta = pull_back(jnp.float32(1.0 / total_cells))
    row_sums = lax.psum(jnp.sum(grad_scale, 1), "gene")
    logit_grad = (grad_scale - jnp.exp(log_scale) * row_sums[:, None]).astype(jnp.bfloat16)
    drop_grad = grad_drop.astype(jnp.bfloat16)
    out_grad = jnp.stack(
        [
            jnp.einsum("ch,cg->hg", gathered, logit_grad, preferred_element_type=jnp.float32),
            jnp.einsum("ch,cg->hg", gathered, drop_grad, preferred_element_type=jnp.float32),
        ]
    )
    gene_grad = jnp.stack(
        [
            jnp.sum(logit_grad.astype(jnp.float32), 0),
            jnp.sum(drop_grad.astype(jnp.float32), 0),
            grad_theta,
        ]
    )
    hidden_grad = lax.psum_scatter(
        jnp.einsum("cg,hg->ch", logit_grad, out_low[0], preferred_element_type=jnp.float32)
        + jnp.einsum("cg,hg->ch", drop_grad, out_low[1], preferred_element_type=jnp.float32),
        "gene",
        scatter_dimension=0,
        tiled=True,
    )
    pre_two_grad, gain_two, shift_two = norm_backward(
        hidden_grad * unit_slope(act_two), normed_two, inv_two, norm_param[2], total_cells
    )
    dec_weight_grad = jnp.einsum(
        "ck,ch->kh", dec_in.astype(jnp.float32), pre_two_grad, precision=HIGHEST
    )
    latent_grad = jnp.einsum(
        "ch,kh->ck", pre_two_grad, dec_low[:L].astype(jnp.float32), precision=HIGHEST
    )
    mean_grad = latent_grad + latent_mean / total_cells
    var_grad = (
        latent_grad * noise_draw * 0.5 * spread + 0.5 * (jnp.exp(log_var) - 1.0) / total_cells
    )
    head_grad_out = jnp.concatenate([mean_grad, var_grad], 1)
    head_weight_grad = jnp.einsum(
        "ch,ck->hk", enc_out.astype(jnp.float32), head_grad_out, precision=HIGHEST
    )
    head_bias_grad = jnp.sum(head_grad_out, 0)
    enc_out_grad = jnp.einsum(
        "ck,hk->ch", head_grad_out, head_low.astype(jnp.float32), precision=HIGHEST
    )
    pre_one_grad, gain_one, shift_one = norm_backward(
        enc_out_grad * unit_slope(act_one), normed_one, inv_one, norm_param[0], total_cells
    )
    all_grad = lax.all_gather(pre_one_grad.astype(jnp.bfloat16), "gene", axis=0, tiled=True)
    enc_grad = jnp.einsum("cg,ch->gh", log_counts, all_grad, preferred_element_type=jnp.float32)
    enc_grad, out_grad, gene_grad = lax.psum((enc_grad, out_grad, gene_grad), "cell")
    norm_grad = jnp.stack([gain_one, shift_one, gain_two, shift_two])
    shard_local = squared(enc_grad) + squared(out_grad) + squared(gene_grad)
    local_loss_sum = recon_sum + kl_sum
    head_weight_grad, head_bias_grad, dec_weight_grad, loss_sum = lax.psum(
        (head_weight_grad, head_bias_grad, dec_weight_grad, local_loss_sum), ("gene", "cell")
    )
    shard_total = lax.psum(shard_local, "gene")
    grad_norm = jnp.sqrt(
        shard_total
        + squared(head_weight_grad)
        + squared(head_bias_grad)
        + squared(dec_weight_grad)
        + squared(norm_grad)
    )
    factor = jnp.minimum(1.0, CLIP_NORM / (grad_norm + 1e-06))
    enc_new = adam_update(enc_weight, enc_first, enc_second, enc_grad * factor, G ** (-0.5))
    out_new = adam_update(out_weight, out_first, out_second, out_grad * factor, H ** (-0.5))
    gene_new = adam_update(gene_param, gene_first, gene_second, gene_grad * factor, 0.3)
    head_new = adam_update(
        head_weight, head_first, head_second, head_weight_grad * factor, H ** (-0.5)
    )
    bias_new = adam_update(head_bias, bias_first, bias_second, head_bias_grad * factor, 0.3)
    dec_new = adam_update(
        dec_weight, dec_first, dec_second, dec_weight_grad * factor, (L + NB) ** (-0.5)
    )
    norm_new = adam_update(norm_param, norm_first, norm_second, norm_grad * factor, 0.3)
    return (
        loss_sum,
        grad_norm,
        enc_new[0],
        enc_new[1],
        enc_new[2],
        out_new[0],
        out_new[1],
        out_new[2],
        gene_new[0],
        gene_new[1],
        gene_new[2],
        head_new[0],
        head_new[1],
        head_new[2],
        bias_new[0],
        bias_new[1],
        bias_new[2],
        dec_new[0],
        dec_new[1],
        dec_new[2],
        norm_new[0],
        norm_new[1],
        norm_new[2],
        enc_new[0].astype(jnp.bfloat16),
        out_new[0].astype(jnp.bfloat16),
        head_new[0].astype(jnp.bfloat16),
        dec_new[0].astype(jnp.bfloat16),
    )


def solution(mesh):
    in_specs = (
        P("cell", "gene"),
        P(("cell", "gene")),
        P(("cell", "gene"), None),
        P("gene", None),
        P("gene", None),
        P("gene", None),
        P(None, None, "gene"),
        P(None, None, "gene"),
        P(None, None, "gene"),
        P(None, "gene"),
        P(None, "gene"),
        P(None, "gene"),
        P(),
        P(),
        P(),
        P(),
        P(),
        P(),
        P(),
        P(),
        P(),
        P(),
        P(),
        P(),
    )
    out_specs = (
        P(),
        P(),
        P("gene", None),
        P("gene", None),
        P("gene", None),
        P(None, None, "gene"),
        P(None, None, "gene"),
        P(None, None, "gene"),
        P(None, "gene"),
        P(None, "gene"),
        P(None, "gene"),
        P(),
        P(),
        P(),
        P(),
        P(),
        P(),
        P(),
        P(),
        P(),
        P(),
        P(),
        P(),
        P("gene", None),
        P(None, None, "gene"),
        P(),
        P(),
    )
    return jax.shard_map(
        per_device, mesh=mesh, in_specs=in_specs, out_specs=out_specs, check_vma=False
    )
```

profile of v0, /device:TPU:0, one launch (start us, length us, event | category | flops | bytes accessed | tf_op | source)
XLA Modules:
  0.0 1312.0 jit_solution(15581640601286144364)
XLA Ops:
  7.2 15.7 %fusion.86 = f32[2048,128]{1,0:T(8,128)} fusion(s32[2048,2500]{0,1:T(8,128)} %param.27, f32[2500,128]{1,0:T(8,128)} %param.30), kind=kOutput, calls=%fused_computation.144 | convolution fusion | flops 1321280000 | bytes 22808576 | tf_op jit(solution)/shard_map/dot_general | solution.py:133
  22.9 5.4 all-to-all-start
  30.7 162.9 %fusion.34 = (f32[2500]{0:T(1024)}, f32[2048]{0:T(1024)S(1)}) fusion(s32[2048,2500]{0,1:T(8,128)} %param.27, f32[2500]{0:T(1024)S(1)} %get-tuple-element.391, f32[2500]{0:T(1024)S(1)} %get-tuple-element.390, f32[2500]{0:T(1024)S(1)} %get-tuple-element.389, f32[2500]{0:T(1024)S(1)} %get-tuple-element.392, pred[2500]{0:T(1024)(128)(4,1)S(1)} %get-tuple-element.385, ...), kind=kLoop, calls=%fused_computation.70 | loop fusion | flops 737275456 | bytes 20543192 | tf_op jit(solution)/shard_map/transpose(jvp())/reduce_sum | solution.py:66
  193.5 9.7 all-gather.2
  203.3 1.3 copy.88
  204.8 1.5 fusion.118
  206.4 40.0 %all-reduce.3 = (f32[128]{0:T(128)S(1)}, f32[128]{0:T(128)S(1)}) all-reduce(f32[128]{0:T(128)S(1)} %multiply_reduce_fusion.8, f32[128]{0:T(128)S(1)} %get-tuple-element.303), channel_id=1, replica_groups=mesh['gene'=8,'cell'=4] {'gene','cell'}, use_global_device_ids=true, to_apply=%region_4.0 | all-reduce | flops 256 | bytes 2048 | tf_op jit(solution)/shard_map/psum | solution.py:42
  248.3 41.0 %all-reduce.2 = (f32[128]{0:T(128)S(1)}, f32[128]{0:T(128)S(1)}) all-reduce(f32[128]{0:T(128)S(1)} %get-tuple-element.310, f32[128]{0:T(128)S(1)} %get-tuple-element.309), channel_id=1, replica_groups=mesh['gene'=8,'cell'=4] {'gene','cell'}, use_global_device_ids=true, to_apply=%region_8.0 | all-reduce | flops 256 | bytes 2048 | tf_op jit(solution)/shard_map/psum | solution.py:42
  289.9 22.7 %all_gather.24 = bf16[2048,128]{1,0:T(8,128)(2,1)S(1)} all-gather(bf16[256,128]{1,0:T(8,128)(2,1)S(1)} %multiply_convert_fusion.1), channel_id=1, replica_groups=mesh['gene'=8,'cell'=4] {'gene'}, dimensions={0}, use_global_device_ids=true | all-gather | bytes 589824 | tf_op jit(solution)/shard_map/all_gather | solution.py:159
  312.6 9.6 add_reduce_fusion
  322.2 8.2 all-gather
  330.5 9.2 exponential_reduce_fusion
  339.7 9.2 all-gather.1
  349.0 0.7 while.19
  349.7 66.5 %convert_reduce_fusion = (f32[2500]{0:T(1024)S(1)}, bf16[2048,2500]{0,1:T(8,128)(2,1)}, f32[2048,2500]{0,1:T(8,128)}, f32[2048,2500]{0,1:T(8,128)}) fusion(f32[2500]{0:T(1024)S(1)} %get-tuple-element.314, s32[2048,2500]{0,1:T(8,128)} %param.27, f32[2048]{0:T(1024)S(1)} %log_add_fusion, f32[2048,2500]{0,1:T(8,128)} %get-tuple-element.405, ...), kind=kOutput, calls=%fused_computation.116 | convolution fusion | flops 1582077440 | bytes 93400848 | tf_op jit(solution)/shard_map/dot_general | solution.py:162
  416.4 46.4 %fusion.135 = (f32[2048]{0:T(1024)S(1)}, f32[2048,2500]{0,1:T(8,128)}) fusion(f32[2500]{0:T(1024)S(1)} %get-tuple-element.312, f32[2048]{0:T(1024)S(1)} %log_add_fusion, f32[2048,2500]{0,1:T(8,128)} %get-tuple-element.405, f32[2500]{0:T(1024)S(1)} %get-tuple-element.315, f32[2048]{0:T(1024)S(1)} %log.6, f32[2048,2500]{0,1:T(8,128)} %get-tuple-element.374, ...), kind=kLoop, calls=%fused_computation.273 | loop fusion | flops 138237952 | bytes 81974576 | tf_op jit(solution)/shard_map/reduce_sum | solution.py:176
  462.8 319.3 %multiply_reduce_fusion.1 = (f32[2500]{0:T(1024)S(1)}, f32[]{:T(128)}, f32[2500]{0:T(1024)S(1)}, f32[2500]{0:T(1024)S(1)}) fusion(f32[2048,2500]{0,1:T(8,128)} %get-tuple-element.374, s32[2048,2500]{0,1:T(8,128)} %param.27, f32[2500]{0:T(1024)S(1)} %copy-done.44, f32[2500]{0:T(1024)S(1)} %get-tuple-element.313, f32[2048]{0:T(1024)S(1)} %log_add_fusion, ...), kind=kLoop, calls=%fused_computation.115 | loop fusion | flops 1039352512 | bytes 82073888 | tf_op jit(solution)/shard_map/transpose(jvp())/reduce_sum | solution.py:61
  782.7 13.4 %psum.124 = f32[2048]{0:T(1024)S(1)} all-reduce(f32[2048]{0:T(1024)S(1)} %get-tuple-element.376), channel_id=1, replica_groups=mesh['gene'=8,'cell'=4] {'gene'}, use_global_device_ids=true, to_apply=%region_18.20 | all-reduce | flops 2048 | bytes 16384 | tf_op jit(solution)/shard_map/psum | solution.py:176
  796.2 14.6 %convert_reduce_fusion.1 = (f32[2500]{0:T(1024)S(1)}, bf16[2048,2500]{0,1:T(8,128)(2,1)S(1)}) fusion(f32[2048,2500]{0,1:T(8,128)} %get-tuple-element.377, f32[2048]{0:T(1024)S(1)} %psum.124, f32[2048]{0:T(1024)S(1)} %log_add_fusion, f32[2048,2500]{0,1:T(8,128)} %get-tuple-element.405, f32[2500]{0:T(1024)S(1)} %get-tuple-element.315), kind=kLoop, calls=%fused_computation.117 | loop fusion | flops 35837500 | bytes 51236384 | tf_op jit(solution)/shard_map/reduce_sum | solution.py:187
  810.8 3.9 copy-done.1
  814.7 3.5 fusion.93
  818.4 4.4 convolution_add_fusion
  822.9 5.6 convolution_bitcast_fusion
  828.6 5.9 convolution_bitcast_fusion.1
  834.4 1.6 pad_maximum_fusion
  836.1 21.0 %reduce-scatter.2.cloned.1.call-done = f32[256,128]{1,0:T(8,128)} async-done(((f32[2048,128]{1,0:T(8,128)}), f32[256,128]{1,0:T(8,128)}) %reduce-scatter.2.cloned.1.call-update) | async-done | bytes 131088 | tf_op jit(solution)/shard_map/reduce_scatter | solution.py:192
  857.1 1.0 fusion.120
  858.1 39.6 %all-reduce.1 = (f32[128]{0:T(128)S(1)}, f32[128]{0:T(128)S(1)}) all-reduce(f32[128]{0:T(128)S(1)} %get-tuple-element.308, f32[128]{0:T(128)S(1)} %get-tuple-element.307), channel_id=1, replica_groups=mesh['gene'=8,'cell'=4] {'gene','cell'}, use_global_device_ids=true, to_apply=%region_23.25 | all-reduce | flops 256 | bytes 2048 | tf_op jit(solution)/shard_map/psum | solution.py:42
  897.7 1.5 multiply_add_fusion.8
  900.5 41.2 %all-reduce = (f32[]{:T(128)}, f32[128]{0:T(128)S(1)}, f32[128]{0:T(128)S(1)}, f32[128,20]{0,1:T(8,128)S(1)}, f32[20]{0:T(128)S(1)}) all-reduce(f32[]{:T(128)S(6)} %add.379, f32[128]{0:T(128)S(1)} %get-tuple-element.306, f32[128]{0:T(128)S(1)} %get-tuple-element.305, ...), channel_id=1, replica_groups=mesh['gene'=8,'cell'=4] {'gene','cell'}, use_global_device_ids=true, to_apply=%region_16.18 | all-reduce | flops 2837 | bytes 22696 | tf_op jit(solution)/shard_map/psum | solution.py:229
  941.7 11.1 all_gather.31
  952.9 14.8 %fusion.87 = f32[2500,128]{1,0:T(8,128)} fusion(bf16[2048,128]{1,0:T(8,128)(2,1)S(1)} %all_gather.31, s32[2048,2500]{0,1:T(8,128)} %param.27), kind=kOutput, calls=%fused_computation.146 | convolution fusion | flops 1320960000 | bytes 22284288 | tf_op jit(solution)/shard_map/cg,ch->gh/dot_general | solution.py:224
  967.9 19.6 %psum.131 = f32[3,2500]{1,0:T(4,128)S(1)} all-reduce(f32[3,2500]{1,0:T(4,128)S(1)} %pad_maximum_fusion.4), channel_id=1, replica_groups=mesh['gene'=8,'cell'=4] {'cell'}, use_global_device_ids=true, to_apply=%region_38.40 | all-reduce | flops 7500 | bytes 60000 | tf_op jit(solution)/shard_map/psum | solution.py:225
  989.3 1.0 fusion.96
  991.0 121.2 %all-reduce.10.cloned.1.call-done = (f32[2500,128]{1,0:T(8,128)}, f32[2,128,2500]{1,2,0:T(8,128)}) async-done(((f32[2500,128]{1,0:T(8,128)}, f32[2,128,2500]{1,2,0:T(8,128)}), (f32[2500,128]{1,0:T(8,128)}, f32[2,128,2500]{1,2,0:T(8,128)})) %all-reduce.10.cloned.1.call-update) | async-done | bytes 3840016 | tf_op jit(solution)/shard_map/psum | solution.py:225
  1112.2 3.0 multiply_reduce_fusion.3
  1115.2 2.2 multiply_reduce_fusion.4
  1119.4 117.4 %all-reduce.8.cloned.1.call-done = f32[138,128]{1,0:T(8,128)} async-done(((f32[138,128]{1,0:T(8,128)}), f32[138,128]{1,0:T(8,128)}) %all-reduce.8.cloned.1.call-update) | async-done | bytes 70672 | tf_op jit(solution)/shard_map/psum | solution.py:229
  1236.8 1.5 multiply_reduce_fusion.9
  1238.3 14.9 %psum.132 = f32[]{:T(128)} all-reduce(f32[]{:T(128)S(6)} %add.386), channel_id=1, replica_groups=mesh['gene'=8,'cell'=4] {'gene'}, use_global_device_ids=true, to_apply=%region_40.42 | all-reduce | flops 1 | bytes 8 | tf_op jit(solution)/shard_map/psum | solution.py:232
  1256.7 4.7 fusion.126
  1261.4 8.9 copy.76
  1270.3 8.8 copy.77
  1279.1 8.8 copy.78
  1287.9 10.2 copy.79
  1298.1 2.8 fusion.129
  1300.9 0.7 multiply_subtract_fusion.3
  1303.4 0.7 fusion.122
  (232 shorter events, 10.7 us)
Async XLA Ops:
  22.9 180.4 %copy-start.15 = (f32[138,128]{1,0:T(8,128)S(1)}, f32[138,128]{1,0:T(8,128)}, u32[]{:S(2)}) copy-start(f32[138,128]{1,0:T(8,128)} %param.45) | copy-start | bytes 211972
  22.9 180.4 %copy-start.2 = (f32[2,128,2500]{1,0,2:T(2,128)S(1)}, f32[2,128,2500]{1,0,2:T(2,128)}, u32[]{:S(2)}) copy-start(f32[2,128,2500]{1,0,2:T(2,128)} %param.33) | copy-start | bytes 7680004
  22.9 181.9 %all-to-all-start = ((f32[8,256,128]{2,1,0:T(8,128)}), f32[8,256,128]{2,1,0:T(8,128)}, u32[]{:S(2)}, u32[]{:S(2)}) async-start(f32[8,256,128]{2,1,0:T(8,128)} %bitcast.56), calls=%async_computation | async-start | bytes 2097152 | tf_op jit(solution)/shard_map/all_to_all | solution.py:134
  28.3 828.7 %reduce-scatter.2.cloned.1.call-start = ((), (), s32[]{:S(2)}) async-start(), calls=%async_computation.2 | async-start | bytes 1179648 | tf_op jit(solution)/shard_map/reduce_scatter | solution.py:192
  30.0 173.2 %copy-start.47 = (f32[2500]{0:T(1024)}, f32[2500]{0:T(1024)S(1)}, u32[]{:S(2)}) copy-start(f32[2500]{0:T(1024)S(1)} %get-tuple-element.389) | copy-start | bytes 30004
  30.0 173.2 %copy-start.49 = (f32[2500]{0:T(1024)}, f32[2500]{0:T(1024)S(1)}, u32[]{:S(2)}) copy-start(f32[2500]{0:T(1024)S(1)} %get-tuple-element.390) | copy-start | bytes 30004
  30.0 173.2 %copy-start.51 = (f32[2500]{0:T(1024)}, f32[2500]{0:T(1024)S(1)}, u32[]{:S(2)}) copy-start(f32[2500]{0:T(1024)S(1)} %get-tuple-element.392) | copy-start | bytes 30004
  30.6 172.6 %copy-start.63 = (pred[2500]{0:T(1024)(128)(4,1)}, pred[2500]{0:T(1024)(128)(4,1)S(1)}, u32[]{:S(2)}) copy-start(pred[2500]{0:T(1024)(128)(4,1)S(1)} %get-tuple-element.384) | copy-start | bytes 7504
  30.6 174.0 %copy-start.35 = (f32[4,128]{1,0:T(4,128)S(1)}, f32[4,128]{1,0:T(4,128)}, u32[]{:S(2)}) copy-start(f32[4,128]{1,0:T(4,128)} %param.48) | copy-start | bytes 6148
  30.6 174.0 %copy-start.75 = (s32[256]{0:T(256)S(1)}, s32[256]{0:T(256)}, u32[]{:S(2)}) copy-start(s32[256]{0:T(256)} %param.28) | copy-start | bytes 3076
  30.6 216.4 %copy-start.30 = (f32[128,20]{0,1:T(8,128)S(1)}, f32[128,20]{0,1:T(8,128)}, u32[]{:S(2)}) copy-start(f32[128,20]{0,1:T(8,128)} %param.39) | copy-start | bytes 30724
  30.7 216.4 %copy-start.67 = (f32[20]{0:T(128)S(1)}, f32[20]{0:T(128)}, u32[]{:S(2)}) copy-start(f32[20]{0:T(128)} %param.42) | copy-start | bytes 244
  30.7 216.5 %copy-start.28 = (f32[256,10]{0,1:T(8,128)S(1)}, f32[256,10]{0,1:T(8,128)}, u32[]{:S(2)}) copy-start(f32[256,10]{0,1:T(8,128)} %param.29) | copy-start | bytes 30724
  203.3 127.1 %copy-start.32 = (bf16[138,128]{1,0:T(8,128)(2,1)}, bf16[138,128]{1,0:T(8,128)(2,1)S(1)}, u32[]{:S(2)}) copy-start(bf16[138,128]{1,0:T(8,128)(2,1)S(1)} %convert_element_type.69) | copy-start | bytes 105988
  204.6 125.8 %copy-start.57 = (f32[128]{0:T(128)}, f32[128]{0:T(128)S(1)}, u32[]{:S(2)}) copy-start(f32[128]{0:T(128)S(1)} %get-tuple-element.395) | copy-start | bytes 1540
  204.7 125.8 %copy-start.59 = (f32[128]{0:T(128)}, f32[128]{0:T(128)S(1)}, u32[]{:S(2)}) copy-start(f32[128]{0:T(128)S(1)} %get-tuple-element.398) | copy-start | bytes 1540
  204.8 85.1 %copy-start.18 = (bf16[256,128]{1,0:T(8,128)(2,1)}, bf16[256,128]{1,0:T(8,128)(2,1)S(1)}, u32[]{:S(2)}) copy-start(bf16[256,128]{1,0:T(8,128)(2,1)S(1)} %fusion.95) | copy-start | bytes 196612
  206.3 83.5 %copy-start.7 = (f32[256,128]{1,0:T(8,128)}, f32[256,128]{1,0:T(8,128)S(1)}, u32[]{:S(2)}) copy-start(f32[256,128]{1,0:T(8,128)S(1)} %get-tuple-element.304) | copy-start | bytes 393220
  289.8 49.9 %copy-start.37 = (f32[128]{0:T(128)}, f32[128]{0:T(128)S(1)}, u32[]{:S(2)}) copy-start(f32[128]{0:T(128)S(1)} %get-tuple-element.399) | copy-start | bytes 1540
  289.8 49.9 %copy-start.39 = (f32[128]{0:T(128)}, f32[128]{0:T(128)S(1)}, u32[]{:S(2)}) copy-start(f32[128]{0:T(128)S(1)} %get-tuple-element.400) | copy-start | bytes 1540
  416.3 46.5 %copy-start.44 = (f32[2500]{0:T(1024)S(1)}, f32[2500]{0:T(1024)}, u32[]{:S(2)}) copy-start(f32[2500]{0:T(1024)} %get-tuple-element.311) | copy-start | bytes 30004
  416.3 46.5 %copy-start.45 = (f32[2500]{0:T(1024)S(1)}, f32[2500]{0:T(1024)}, u32[]{:S(2)}) copy-start(f32[2500]{0:T(1024)} %get-tuple-element.387) | copy-start | bytes 30004
  416.3 46.5 %copy-start.46 = (f32[2500]{0:T(1024)S(1)}, f32[2500]{0:T(1024)}, u32[]{:S(2)}) copy-start(f32[2500]{0:T(1024)} %get-tuple-element.388) | copy-start | bytes 30004
  416.3 46.5 %copy-start.48 = (f32[2500]{0:T(1024)S(1)}, f32[2500]{0:T(1024)}, u32[]{:S(2)}) copy-start(f32[2500]{0:T(1024)} %copy-done.47) | copy-start | bytes 30004
  416.3 46.5 %copy-start.50 = (f32[2500]{0:T(1024)S(1)}, f32[2500]{0:T(1024)}, u32[]{:S(2)}) copy-start(f32[2500]{0:T(1024)} %copy-done.49) | copy-start | bytes 30004
  416.3 46.5 %copy-start.52 = (f32[2500]{0:T(1024)S(1)}, f32[2500]{0:T(1024)}, u32[]{:S(2)}) copy-start(f32[2500]{0:T(1024)} %copy-done.51) | copy-start | bytes 30004
  818.3 79.4 %copy-start.23 = (f32[256,20]{0,1:T(8,128)S(1)}, f32[256,20]{0,1:T(8,128)}, u32[]{:S(2)}) copy-start(f32[256,20]{0,1:T(8,128)} %copy-done.22) | copy-start | bytes 61444
  818.3 79.4 %copy-start.29 = (f32[256,10]{0,1:T(8,128)S(1)}, f32[256,10]{0,1:T(8,128)}, u32[]{:S(2)}) copy-start(f32[256,10]{0,1:T(8,128)} %param.29) | copy-start | bytes 30724
  818.3 79.4 %copy-start.61 = (f32[128]{0:T(128)S(1)}, f32[128]{0:T(128)}, u32[]{:S(2)}) copy-start(f32[128]{0:T(128)} %get-tuple-element.394) | copy-start | bytes 1540
  818.3 80.9 %copy-start.8 = (f32[256,128]{1,0:T(8,128)S(1)}, f32[256,128]{1,0:T(8,128)}, u32[]{:S(2)}) copy-start(f32[256,128]{1,0:T(8,128)} %copy-done.7) | copy-start | bytes 393220
  818.3 80.9 %copy-start.31 = (f32[128,20]{0,1:T(8,128)S(1)}, f32[128,20]{0,1:T(8,128)}, u32[]{:S(2)}) copy-start(f32[128,20]{0,1:T(8,128)} %param.39) | copy-start | bytes 30724
  818.3 80.9 %copy-start.54 = (f32[128]{0:T(128)S(1)}, f32[128]{0:T(128)}, u32[]{:S(2)}) copy-start(f32[128]{0:T(128)} %copy-done.53) | copy-start | bytes 1540
  818.4 80.8 %copy-start.56 = (f32[128]{0:T(128)S(1)}, f32[128]{0:T(128)}, u32[]{:S(2)}) copy-start(f32[128]{0:T(128)} %copy-done.55) | copy-start | bytes 1540
  818.4 80.8 %copy-start.70 = (f32[128]{0:T(128)S(1)}, f32[128]{0:T(128)}, u32[]{:S(2)}) copy-start(f32[128]{0:T(128)} %copy-done.69) | copy-start | bytes 1540
  818.4 80.8 %copy-start.72 = (f32[128]{0:T(128)S(1)}, f32[128]{0:T(128)}, u32[]{:S(2)}) copy-start(f32[128]{0:T(128)} %copy-done.71) | copy-start | bytes 1540
  818.4 81.2 %copy-start.14 = (bf16[256,128]{1,0:T(8,128)(2,1)S(1)}, bf16[256,128]{1,0:T(8,128)(2,1)}, u32[]{:S(2)}) copy-start(bf16[256,128]{1,0:T(8,128)(2,1)} %copy-done.13) | copy-start | bytes 196612
  818.4 123.3 %copy-start.66 = (f32[128]{0:T(128)S(1)}, f32[128]{0:T(128)}, u32[]{:S(2)}) copy-start(f32[128]{0:T(128)} %get-tuple-element.393) | copy-start | bytes 1540
  822.8 289.4 %all-reduce.10.cloned.1.call-start = ((), (), s32[]{:S(2)}) async-start(), calls=%async_computation.4 | async-start | bytes 7692288 | tf_op jit(solution)/shard_map/psum | solution.py:225
  828.5 139.3 %copy-start.41 = (f32[2500]{0:T(1024)S(1)}, f32[2500]{0:T(1024)}, u32[]{:S(2)}) copy-start(f32[2500]{0:T(1024)} %get-tuple-element.301) | copy-start | bytes 30004
  828.5 139.3 %copy-start.25 = (f32[3,2500]{1,0:T(4,128)S(1)}, f32[3,2500]{1,0:T(4,128)}, u32[]{:S(2)}) copy-start(f32[3,2500]{1,0:T(4,128)} %param.36) | copy-start | bytes 90004
  828.5 160.8 %copy-start.19 = (bf16[256,128]{1,0:T(8,128)(2,1)S(1)}, bf16[256,128]{1,0:T(8,128)(2,1)}, u32[]{:S(2)}) copy-start(bf16[256,128]{1,0:T(8,128)(2,1)} %copy-done.18) | copy-start | bytes 196612
  828.5 160.8 %copy-start.21 = (bf16[256,10]{1,0:T(8,128)(2,1)S(1)}, bf16[256,10]{1,0:T(8,128)(2,1)}, u32[]{:S(2)}) copy-start(bf16[256,10]{1,0:T(8,128)(2,1)} %copy-done.20) | copy-start | bytes 15364
  834.4 422.0 %copy-start.3 = (f32[2,128,2500]{1,0,2:T(2,128)S(1)}, f32[2,128,2500]{1,0,2:T(2,128)}, u32[]{:S(2)}) copy-start(f32[2,128,2500]{1,0,2:T(2,128)} %param.33) | copy-start | bytes 7680004
  967.7 269.1 %all-reduce.8.cloned.1.call-start = ((), (), s32[]{:S(2)}) async-start(), calls=%async_computation.3 | async-start | bytes 147456 | tf_op jit(solution)/shard_map/psum | solution.py:229
  1256.6 46.8 %copy-start.16 = (f32[138,128]{1,0:T(8,128)S(1)}, f32[138,128]{1,0:T(8,128)}, u32[]{:S(2)}) copy-start(f32[138,128]{1,0:T(8,128)} %param.45) | copy-start | bytes 211972
  1256.6 46.8 %copy-start.17 = (f32[138,128]{1,0:T(8,128)S(1)}, f32[138,128]{1,0:T(8,128)}, u32[]{:S(2)}) copy-start(f32[138,128]{1,0:T(8,128)} %all-reduce.8.cloned.1.call-done) | copy-start | bytes 211972
  1256.7 46.7 %copy-start.26 = (f32[138,128]{1,0:T(8,128)S(1)}, f32[138,128]{1,0:T(8,128)}, u32[]{:S(2)}) copy-start(f32[138,128]{1,0:T(8,128)} %param.46) | copy-start | bytes 211972
  1256.7 46.7 %copy-start.27 = (f32[138,128]{1,0:T(8,128)S(1)}, f32[138,128]{1,0:T(8,128)}, u32[]{:S(2)}) copy-start(f32[138,128]{1,0:T(8,128)} %param.47) | copy-start | bytes 211972
  (34 other events, 1208.3 us)
Sparse Core Ops, SparseCore 0:
  822.9 34.0 reduce-scatter.1
  967.8 144.3 all-reduce.9
  1119.3 117.4 all-reduce.7
where the time goes:
time: 1320 us; the launch traced here: 1310 us
  other arithmetic  579 us (44%)
  blocking collectives  271 us (21%)
  waiting for transfers between devices  260 us (20%)
  matrix products  129 us (10%)
  local copies, waits for them, and re-layouts  43.8 us (3%)
  between operations  22.7 us (2%)
    reduce_sum x1, other arithmetic, zinb_terms(): log_both = jnp.logaddexp(log_theta, log_mean)  319 us
    reduce_sum x1, other arithmetic, zinb_terms(): theta_full = jnp.broadcast_to(theta, fcounts.shape)  163 us
    psum x1, waiting for transfers between devices, per_device(): lax.psum((enc_grad, out_grad, gene_grad), 'cell')  121 us
    psum x3, blocking collectives, moments_sum(): return lax.psum((first_part, second_part), ('gene', 'cell'))  121 us
    psum x1, waiting for transfers between devices, per_device(): lax.psum((head_weight_grad, head_bias_grad, dec_weight_grad, local_loss_s...  117 us
    dot_general x1, matrix products, per_device(): jnp.dot(gathered, out_low[1], preferred_element_type=jnp.float32)  66.5 us
    reduce_sum x1, other arithmetic, per_device(): row_sums = lax.psum(jnp.sum(grad_scale, 1), 'gene')  46.4 us
    unnamed x161, local copies, waits for them, and re-layouts  43.4 us
  transfers between devices with their start and end apart: 4, of which 3 were waited for; matrix products, arithmetic and copies ran while one was open for 14% of the time, Pallas kernels for 0%

commit v1 on v0

v1 whole, which is shorter than its diff:
```python
import jax
import jax.numpy as jnp
from jax import lax
from jax.experimental import pallas as pl
from jax.experimental.pallas import tpu as pltpu
from jax.sharding import PartitionSpec as P

L = 10
NB = 128
STEP = 10
G = 20000
H = 128
BETA_ONE = 0.9
BETA_TWO = 0.999
ADAM_EPS = 1e-08
DECAY_RATE = 0.01
CLIP_NORM = 0.25
NORM_EPS = 0.001
TOP_COUNT = 16
LOG2E = 1.4426950408889634
LN2 = 0.6931471805599453
DROP_TOP = 60.0
FAR_DOWN = -1e30
KA = 144
CELL_BLOCK = 256
LANE_BLOCK = 512
F32 = jnp.float32
BF16 = jnp.bfloat16
VMEM_BYTES = 56 * 2**20


def round_up(value, unit):
    return -(-value // unit) * unit


def gene_tile(padded):
    return 256 if padded % 256 == 0 else 128


def turned_block(block, devices, per_device_blocks):
    owner = block // per_device_blocks
    out = 0
    bit = 1
    while bit < devices:
        out = 2 * out + (owner // bit) % 2
        bit *= 2
    return out * per_device_blocks + block % per_device_blocks


def params(flops=0, read=0):
    return dict(
        compiler_params=pltpu.CompilerParams(vmem_limit_bytes=VMEM_BYTES),
        cost_estimate=pl.CostEstimate(flops=flops, bytes_accessed=read, transcendentals=0),
    )


def dot(left, right):
    return jnp.dot(left, right, preferred_element_type=F32)


def dot_nt(left, right):
    return lax.dot_general(left, right, (((1,), (1,)), ((), ())), preferred_element_type=F32)


def dot_tn(left, right):
    return lax.dot_general(left, right, (((0,), (0,)), ((), ())), preferred_element_type=F32)


def two_parts(value):
    high = value.astype(BF16)
    return high, (value - high.astype(F32)).astype(BF16)


def as_column(row, lanes):
    square = jnp.transpose(jnp.broadcast_to(row, (128, 128)))
    return jnp.concatenate([square] * (lanes // 128), axis=1)


def lane_sums_row(value):
    total = value[:, :128]
    for k in range(1, value.shape[1] // 128):
        total = total + value[:, k * 128 : (k + 1) * 128]
    return jnp.sum(jnp.transpose(total), axis=0, keepdims=True)


def stack_rows(rows):
    wide = rows[0].shape[1]
    index = lax.broadcasted_iota(jnp.int32, (8, wide), 0)
    out = jnp.zeros((8, wide), F32)
    for k, row in enumerate(rows):
        out = jnp.where(index == k, jnp.broadcast_to(row, (8, wide)), out)
    return out


def sigmoid(value):
    return 1.0 / (1.0 + jnp.exp(-value))


def log_counts(block, first_row, genes):
    if first_row + block.shape[0] > genes:
        row = lax.broadcasted_iota(jnp.int32, block.shape, 0) + first_row
        block = jnp.where(row < genes, block, 0)
    value = block.astype(F32)
    return value, (jnp.log2(value + 1.0) * LN2).astype(BF16)


def encoder_sums(counts, enc_weight, place):
    genes, cells = counts.shape
    padded = round_up(genes, 128)
    tile = gene_tile(padded)
    tc = CELL_BLOCK

    def kernel(cnt_ref, w_ref, out_ref, tot_ref, wlow, xs):
        @pl.when(pl.program_id(0) == 0)
        def _():
            for k in range(padded // 128):
                rows = lax.broadcasted_iota(jnp.int32, (128, 128), 0) + k * 128
                part = jnp.where(rows < genes, w_ref[k * 128 : (k + 1) * 128, :], 0.0)
                wlow[:, k * 128 : (k + 1) * 128] = jnp.transpose(part).astype(BF16)

        total = jnp.zeros((8, tc), F32)
        out = jnp.zeros((128, tc), F32)
        for j in range(padded // tile):
            for r in range(0, tile, 16):
                at = slice(j * tile + r, j * tile + r + 16)
                value, low = log_counts(cnt_ref[at, :], j * tile + r, genes)
                xs[at, :] = low
                total = total + (value[0:8] + value[8:16])
            span = slice(j * tile, (j + 1) * tile)
            out = out + dot(wlow[:, span], xs[span, :])
        out_ref[...] = out
        tot_ref[...] = jnp.broadcast_to(jnp.sum(total, axis=0, keepdims=True), (8, tc))

    return pl.pallas_call(
        kernel,
        grid=(cells // tc,),
        in_specs=[
            pl.BlockSpec((padded, tc), lambda i: (0, i)),
            pl.BlockSpec((padded, 128), lambda i: (0, 0)),
        ],
        out_specs=[
            pl.BlockSpec((128, tc), lambda i: (0, place(i))),
            pl.BlockSpec((8, tc), lambda i: (0, place(i))),
        ],
        out_shape=[
            jax.ShapeDtypeStruct((128, cells), F32),
            jax.ShapeDtypeStruct((8, cells), F32),
        ],
        scratch_shapes=[
            pltpu.VMEM((128, padded), BF16),
            pltpu.VMEM((padded, tc), BF16),
        ],
        name="encoder_sums",
        **params(2 * cells * padded * 128, 4 * cells * padded),
    )(counts, enc_weight)


def three_parts(value):
    high = value.astype(BF16).astype(F32)
    middle = (value - high).astype(BF16).astype(F32)
    return high, middle, value - high - middle


def decoder_weights(out_rows, gene_param):
    genes = gene_param.shape[1]
    padded = round_up(genes, 128)
    tile = gene_tile(padded)

    def kernel(
        w_ref, gene_ref, wy_ref, wd_ref, zero_ref, one_ref, mixed_ref, theta_ref, sum_ref, slope_ref
    ):
        first = pl.program_id(0) * tile
        row = lax.broadcasted_iota(jnp.int32, (tile, 128), 0) + first
        lane = lax.broadcasted_iota(jnp.int32, (tile, 128), 1)
        inside = row < genes
        zero = jnp.where(inside, w_ref[pl.ds(0, tile, stride=2), :], 0.0)
        one = jnp.where(inside, w_ref[pl.ds(1, tile, stride=2), :], 0.0)
        low_zero = zero.astype(BF16)
        turned = jnp.transpose(jnp.concatenate([gene_ref[...], jnp.zeros((125, tile), F32)], 0))

        def column(k, outside):
            wide = jnp.broadcast_to(turned[:, k : k + 1], (tile, 128))
            return jnp.where(inside, wide, outside)

        bias = column(0, FAR_DOWN)
        drop_bias = column(1, 0.0)
        log_theta = column(2, 0.0)
        theta = jnp.exp(log_theta)

        def pieces(value, at, out):
            for k, part in enumerate(three_parts(value)):
                out = jnp.where(lane == at + k, part, out)
            return out

        ones = jnp.where((lane >= 3) & (lane < 6), 1.0, 0.0)
        side = pieces(log_theta, 6, pieces(bias - log_theta, 0, ones))
        wy_ref[:, 0:128] = low_zero
        wy_ref[:, 128:256] = side.astype(BF16)
        wd_ref[:, 0:128] = one.astype(BF16)
        wd_ref[:, 128:256] = pieces(drop_bias, 0, jnp.zeros((tile, 128), F32)).astype(BF16)
        zero_ref[0:128, :] = jnp.transpose(zero).astype(BF16)
        one_ref[0:128, :] = jnp.transpose(one).astype(BF16)
        across = lax.broadcasted_iota(jnp.int32, (16, tile), 1) + first
        below = lax.broadcasted_iota(jnp.int32, (16, tile), 0)
        zero_ref[128:144, :] = jnp.where((across < genes) & (below == 0), 1.0, 0.0).astype(BF16)
        one_ref[128:144, :] = jnp.zeros((16, tile), BF16)
        mixed_ref[...] = jnp.transpose(low_zero.astype(F32) * theta).astype(BF16)
        theta_ref[...] = theta
        number = lane.astype(F32)
        known = lane < TOP_COUNT
        steps = jnp.where(known, jnp.log2((theta + number) / (number + 1.0)), 0.0)
        slopes = jnp.where(known, (1.0 / LN2) / (theta + number), 0.0)
        index = lax.broadcasted_iota(jnp.int32, (128, 128), 0)
        other = lax.broadcasted_iota(jnp.int32, (128, 128), 1)
        before = jnp.where(index < other, 1.0, 0.0).astype(BF16)

        def running(value):
            out = jnp.zeros((tile, 128), F32)
            for part in three_parts(value):
                out = out + dot(part.astype(BF16), before)
            return out

        sum_ref[...] = running(steps)
        slope_ref[...] = running(slopes)

    shape = jax.ShapeDtypeStruct
    down = lambda j: (j, 0)
    right = lambda j: (0, j)
    return pl.pallas_call(
        kernel,
        grid=(padded // tile,),
        in_specs=[pl.BlockSpec((2 * tile, 128), down), pl.BlockSpec((3, tile), right)],
        out_specs=[
            pl.BlockSpec((tile, 256), down),
            pl.BlockSpec((tile, 256), down),
            pl.BlockSpec((144, tile), right),
            pl.BlockSpec((144, tile), right),
            pl.BlockSpec((128, tile), right),
            pl.BlockSpec((tile, 128), down),
            pl.BlockSpec((tile, 128), down),
            pl.BlockSpec((tile, 128), down),
        ],
        out_shape=[
            shape((padded, 256), BF16),
            shape((padded, 256), BF16),
            shape((144, padded), BF16),
            shape((144, padded), BF16),
            shape((128, padded), BF16),
            shape((padded, 128), F32),
            shape((padded, 128), F32),
            shape((padded, 128), F32),
        ],
        name="decoder_weights",
        **params(100 * 128 * padded, 20 * 128 * padded),
    )(out_rows, gene_param)


def norm_rows(sums, gain, total):
    average = sums[0:1] * (1.0 / total)
    variance = sums[1:2] * (1.0 / total) - average * average
    return average, lax.rsqrt(variance + NORM_EPS)


def hidden_stats(hidden):
    cells = hidden.shape[1]
    block = min(cells, 1024)

    def kernel(h_ref, out_ref):
        one = jnp.zeros((128, 128), F32)
        two = jnp.zeros((128, 128), F32)
        for k in range(block // 128):
            value = h_ref[:, k * 128 : (k + 1) * 128].astype(F32)
            one = one + value
            two = two + value * value
        rows = stack_rows([lane_sums_row(one), lane_sums_row(two)])

        @pl.when(pl.program_id(0) == 0)
        def _():
            out_ref[...] = rows

        @pl.when(pl.program_id(0) > 0)
        def _():
            out_ref[...] += rows

    return pl.pallas_call(
        kernel,
        grid=(cells // block,),
        in_specs=[pl.BlockSpec((128, block), lambda i: (0, i))],
        out_specs=pl.BlockSpec((8, 128), lambda i: (0, 0)),
        out_shape=jax.ShapeDtypeStruct((8, 128), F32),
        name="hidden_stats",
        **params(4 * cells * 128, 2 * cells * 128),
    )(hidden)


def head_terms(h, sums, norm_ref, head_ref, bias_ref, noise, total, lanes):
    average, inv = norm_rows(sums, None, total)
    normed = (h.astype(F32) - as_column(average, lanes)) * as_column(inv, lanes)
    act = normed * as_column(norm_ref[0:1], lanes) + as_column(norm_ref[1:2], lanes)
    gate = sigmoid(act)
    enc_out = (act * gate).astype(BF16)
    head_out = dot(head_ref[...], enc_out) + bias_ref[:, 0:1]
    mean = head_out[0:16]
    log_var = head_out[16:32]
    spread = jnp.exp(0.5 * log_var)
    latent = mean + spread * noise
    return normed, act, gate, enc_out, mean, log_var, spread, latent


def unpack_extra(extra):
    noise = extra[0:16].astype(F32) + extra[16:32].astype(F32)
    label = noise[10:11]
    row = lax.broadcasted_iota(jnp.int32, noise.shape, 0)
    return jnp.where(row < L, noise, 0.0), label


def decoder_input(latent, label):
    index = lax.broadcasted_iota(jnp.int32, (128, label.shape[1]), 0).astype(F32)
    onehot = jnp.where(index == label, 1.0, 0.0).astype(BF16)
    return jnp.concatenate([latent.astype(BF16), onehot], axis=0)


def encoder_heads(gathered, sums, norm_param, head_low, head_bias, dec_low, total):
    cells = gathered.shape[1]
    block = min(cells, LANE_BLOCK)

    def kernel(g_ref, s_ref, norm_ref, head_ref, bias_ref, dec_ref, pre_ref, out_ref):
        noise, label = unpack_extra(g_ref[128:160, :])
        terms = head_terms(
            g_ref[0:128, :], s_ref[...], norm_ref, head_ref, bias_ref, noise, total, block
        )
        mean, log_var, latent = terms[4], terms[5], terms[7]
        pre = dot_tn(dec_ref[...], decoder_input(latent, label))
        pre_ref[...] = pre
        diverge = mean * mean + jnp.exp(log_var) - log_var - 1.0
        kl_row = diverge[0:8, 0:128] + diverge[8:16, 0:128]
        for k in range(1, block // 128):
            span = slice(k * 128, (k + 1) * 128)
            kl_row = kl_row + diverge[0:8, span] + diverge[8:16, span]
        kl_row = 0.5 * jnp.sum(kl_row, axis=0, keepdims=True)
        rows = stack_rows([lane_sums_row(pre), lane_sums_row(pre * pre), kl_row])

        @pl.when(pl.program_id(0) == 0)
        def _():
            out_ref[...] = rows

        @pl.when(pl.program_id(0) > 0)
        def _():
            out_ref[...] += rows

    whole = lambda i: (0, 0)
    return pl.pallas_call(
        kernel,
        grid=(cells // block,),
        in_specs=[
            pl.BlockSpec((160, block), lambda i: (0, i)),
            pl.BlockSpec((8, 128), whole),
            pl.BlockSpec((4, 128), whole),
            pl.BlockSpec((32, 128), whole),
            pl.BlockSpec((32, 128), whole),
            pl.BlockSpec((144, 128), whole),
        ],
        out_specs=[pl.BlockSpec((128, block), lambda i: (0, i)), pl.BlockSpec((8, 128), whole)],
        out_shape=[
            jax.ShapeDtypeStruct((128, cells), F32),
            jax.ShapeDtypeStruct((8, 128), F32),
        ],
        name="encoder_heads",
        **params(2 * cells * 128 * 180, 8 * cells * 128),
    )(gathered, sums, norm_param, head_low, head_bias, dec_low)


def decoder_scan(pre, sums, norm_param, tot_rows, wy, total, devices):
    cells = pre.shape[1]
    padded = wy.shape[0]
    tile = gene_tile(padded)
    tiles = padded // tile
    tc = 2 * CELL_BLOCK

    def kernel(pre_ref, s_ref, norm_ref, tot_ref, wy_ref, hid_ref, turned_ref, rows_ref, rhs, raw):
        average, inv = norm_rows(s_ref[...], None, total)
        scale = inv * norm_ref[2:3]
        offset = norm_ref[3:4] - average * scale
        act = pre_ref[...] * as_column(scale, tc) + as_column(offset, tc)
        hidden = act * sigmoid(act)
        low = hidden.astype(BF16)
        turned_ref[...] = low
        hid_ref[...] = jnp.transpose(hidden).astype(BF16)
        rhs[0:128, :] = low
        index = lax.broadcasted_iota(jnp.int32, (128, tc), 0)
        used = (index < 3) | ((index >= 6) & (index < 9))
        rhs[128:256, :] = jnp.where(used, 1.0, 0.0).astype(BF16)

        def logits(j):
            raw[j % 2] = dot(wy_ref[j * tile : (j + 1) * tile, :], rhs[...])

        logits(0)
        top = jnp.full((8, tc), 4.0 * FAR_DOWN, F32)
        exp_sum = jnp.zeros((8, tc), F32)
        for j in range(tiles):
            if j + 1 < tiles:
                logits(j + 1)
            best = top
            for r in range(0, tile, 8):
                best = jnp.maximum(best, raw[j % 2, r : r + 8, :])
            down = best * LOG2E
            exp_sum = exp_sum * jnp.exp2(top * LOG2E - down)
            for r in range(0, tile, 8):
                exp_sum = exp_sum + jnp.exp2(raw[j % 2, r : r + 8, :] * LOG2E - down)
            top = best
        highest = jnp.max(top, axis=0, keepdims=True)
        merged = jnp.sum(exp_sum * jnp.exp(top - highest), axis=0, keepdims=True)
        rows = stack_rows([highest + jnp.log(merged), tot_ref[0:1, :]])[0:2]
        for k in range(devices):
            rows_ref[k] = rows

    whole = lambda i: (0, 0)
    return pl.pallas_call(
        kernel,
        grid=(cells // tc,),
        in_specs=[
            pl.BlockSpec((128, tc), lambda i: (0, i)),
            pl.BlockSpec((8, 128), whole),
            pl.BlockSpec((4, 128), whole),
            pl.BlockSpec((8, tc), lambda i: (0, i)),
            pl.BlockSpec((padded, 256), whole),
        ],
        out_specs=[
            pl.BlockSpec((tc, 128), lambda i: (i, 0)),
            pl.BlockSpec((128, tc), lambda i: (0, i)),
            pl.BlockSpec((devices, 2, tc), lambda i: (0, 0, i)),
        ],
        out_shape=[
            jax.ShapeDtypeStruct((cells, 128), BF16),
            jax.ShapeDtypeStruct((128, cells), BF16),
            jax.ShapeDtypeStruct((devices, 2, cells), F32),
        ],
        scratch_shapes=[
            pltpu.VMEM((256, tc), BF16),
            pltpu.VMEM((2, tile, tc), F32),
        ],
        name="decoder_scan",
        **params(2 * cells * padded * 128, 4 * cells * 128),
    )(pre, sums, norm_param, tot_rows, wy)


def combine_rows(rows_ref):
    count = rows_ref.shape[0]
    top = rows_ref[0, 0:1, :]
    for k in range(1, count):
        top = jnp.maximum(top, rows_ref[k, 0:1, :])
    exp_sum = jnp.zeros_like(top)
    total = jnp.zeros_like(top)
    for k in range(count):
        exp_sum = exp_sum + jnp.exp(rows_ref[k, 0:1, :] - top)
        total = total + rows_ref[k, 1:2, :]
    return top + jnp.log(exp_sum), total


def decoder_grads(counts, hidden, turned, rows, weights, place):
    wy, wd, zero, one, mixed, theta, sums, slopes = weights
    genes, cells = counts.shape
    padded = theta.shape[0]
    tile = gene_tile(padded)
    tiles = padded // tile
    half = CELL_BLOCK
    tc = 2 * half
    devices = rows.shape[0]

    def kernel(
        cnt_a, cnt_b, hid_ref, turned_ref, rows_ref, wy_ref, wd_ref, zero_ref, one_ref, mixed_ref,
        theta_ref, table_ref, slope_ref,
        x_ref, back_ref, mix_ref, sum_ref, scale_ref, drop_ref, col_ref, loss_ref,
        rhs, right, raw, scale_s, drop_s, acc, mix,
    ):
        @pl.when(pl.program_id(0) == 0)
        def _():
            scale_ref[...] = jnp.zeros(scale_ref.shape, F32)
            drop_ref[...] = jnp.zeros(drop_ref.shape, F32)
            col_ref[...] = jnp.zeros(col_ref.shape, F32)
            loss_ref[...] = jnp.zeros(loss_ref.shape, F32)

        lse, total = combine_rows(rows_ref)
        index = lax.broadcasted_iota(jnp.int32, (128, tc), 0)
        extra = jnp.where(index < 3, 1.0, 0.0)
        for k, row in enumerate(three_parts(jnp.log(total) - lse)):
            extra = jnp.where(index == k + 3, jnp.broadcast_to(row, (128, tc)), extra)
        rhs[0:128, :] = turned_ref[...]
        rhs[128:256, :] = extra.astype(BF16)
        right[:, 0:128] = hid_ref[...]
        lane = lax.broadcasted_iota(jnp.int32, (tc, 128), 1)
        right[:, 128:256] = jnp.where(lane == 0, 1.0, 0.0).astype(BF16)
        acc[...] = jnp.zeros(acc.shape, F32)
        mix[...] = jnp.zeros(mix.shape, F32)

        def rows_of(j):
            if isinstance(j, int):
                return pl.ds(j * tile, tile)
            return pl.ds(pl.multiple_of(j * tile, tile), tile)

        def products(j, slot):
            at = rows_of(j)
            raw[slot, 0:tile, :] = dot(wy_ref[at, :], rhs[...])
            raw[slot, tile : 2 * tile, :] = dot(wd_ref[at, :], rhs[...])

        def entries(j, slot, loss_acc, edge):
            base = j * tile
            for r in range(0, tile, 16):
                if isinstance(base, int):
                    at = pl.ds(base + r, 16)
                else:
                    at = pl.ds(pl.multiple_of(base + r, 16), 16)
                theta = theta_ref[at, :]
                theta = jnp.concatenate([theta, theta], 1)
                table = table_ref[at, :]
                slope_table = slope_ref[at, :]
                col = jnp.zeros((16, 128), F32)
                for side, cnt_ref in enumerate((cnt_a, cnt_b)):
                    span = slice(side * half, (side + 1) * half)
                    number = cnt_ref[at, :]
                    if edge and base + r + 16 > genes:
                        row = lax.broadcasted_iota(jnp.int32, number.shape, 0) + base + r
                        number = jnp.where(row < genes, number, 0)
                    y2 = raw[slot, r : r + 16, span] * LOG2E
                    d2 = raw[slot, tile + r : tile + r + 16, span] * LOG2E
                    held = jnp.minimum(d2, DROP_TOP)
                    x = jnp.exp2(y2)
                    x_one = 1.0 + x
                    lg = jnp.log2(x_one)
                    rc = pltpu.reciprocal(x_one, approx=True)
                    lift = theta * lg
                    keep = pltpu.reciprocal(1.0 + jnp.exp2(held), approx=True)
                    w_one = 1.0 + jnp.exp2(held + lift)
                    z = pltpu.reciprocal(w_one, approx=True)
                    none = number == 0
                    z = jnp.where(none, z, 1.0)
                    value = number.astype(F32)
                    zt = z * theta
                    x_ref[at, span] = x.astype(BF16)
                    scale_s[slot, r : r + 16, span] = (rc * (value + zt) - zt).astype(BF16)
                    drop_s[slot, r : r + 16, span] = (keep - z).astype(BF16)
                    like = jnp.log2(keep * jnp.where(none, w_one, 1.0)) - lift
                    like = like + value * (y2 - lg)
                    like = like + jnp.where(none, 0.0, held - d2)
                    loss_acc = loss_acc + (like[0:8] + like[8:16])
                    slope = z * lg
                    picked = []
                    for k in range(0, half, 128):
                        at_lane = number[:, k : k + 128]
                        picked.append(
                            jnp.take_along_axis(table, at_lane, axis=1, mode="promise_in_bounds")
                        )
                        col = col + (
                            jnp.take_along_axis(slope_table, at_lane, axis=1, mode="promise_in_bounds")
                            - slope[:, k : k + 128]
                        )
                    picked = jnp.concatenate(picked, 1)
                    loss_acc = loss_acc + (picked[0:8] + picked[8:16])
                col_ref[at, :] += col
            return loss_acc

        def gradients(j, slot):
            at = rows_of(j)
            scale_v = scale_s[slot]
            drop_v = drop_s[slot]
            acc[...] += dot(zero_ref[:, at], scale_v) + dot(one_ref[:, at], drop_v)
            mix[...] += dot(mixed_ref[:, at], x_ref[at, :])
            scale_ref[at, :] += dot(scale_v, right[...])
            drop_ref[at, :] += dot(drop_v, right[...])

        products(tiles - 1, 0)
        products(0, 1)
        loss_acc = entries(tiles - 1, 0, jnp.zeros((8, half), F32), True)

        def body(j, loss_acc):
            slot = lax.rem(j + 1, 2)
            products(jnp.minimum(j + 1, tiles - 2), 1 - slot)
            gradients(jnp.where(j == 0, tiles - 1, j - 1), 1 - slot)
            return entries(j, slot, loss_acc, False)

        loss_acc = lax.fori_loop(0, tiles - 1, body, loss_acc)
        gradients(tiles - 2, (tiles - 1) % 2)
        loss_ref[...] += loss_acc[:, 0:128] + loss_acc[:, 128:256]
        back_ref[...] = acc[0:128, :]
        for k in range(devices):
            sum_ref[k] = acc[128:129, :]
        mix_ref[...] = mix[...] * (1.0 / total)

    whole = lambda i: (0, 0)
    across = lambda i: (0, i)
    shape = jax.ShapeDtypeStruct
    return pl.pallas_call(
        kernel,
        grid=(cells // tc,),
        in_specs=[
            pl.BlockSpec((padded, half), lambda i: (0, place(2 * i))),
            pl.BlockSpec((padded, half), lambda i: (0, place(2 * i + 1))),
            pl.BlockSpec((tc, 128), lambda i: (i, 0)),
            pl.BlockSpec((128, tc), across),
            pl.BlockSpec((devices, 2, tc), lambda i: (0, 0, i)),
            pl.BlockSpec((padded, 256), whole),
            pl.BlockSpec((padded, 256), whole),
            pl.BlockSpec((144, padded), whole),
            pl.BlockSpec((144, padded), whole),
            pl.BlockSpec((128, padded), whole),
            pl.BlockSpec((padded, 128), whole),
            pl.BlockSpec((padded, 128), whole),
            pl.BlockSpec((padded, 128), whole),
        ],
        out_specs=[
            pl.BlockSpec((padded, tc), across),
            pl.BlockSpec((128, tc), across),
            pl.BlockSpec((128, tc), across),
            pl.BlockSpec((devices, 1, tc), lambda i: (0, 0, i)),
            pl.BlockSpec((padded, 256), whole),
            pl.BlockSpec((padded, 256), whole),
            pl.BlockSpec((padded, 128), whole),
            pl.BlockSpec((8, 128), whole),
        ],
        out_shape=[
            shape((padded, cells), BF16),
            shape((128, cells), F32),
            shape((128, cells), F32),
            shape((devices, 1, cells), F32),
            shape((padded, 256), F32),
            shape((padded, 256), F32),
            shape((padded, 128), F32),
            shape((8, 128), F32),
        ],
        scratch_shapes=[
            pltpu.VMEM((256, tc), BF16),
            pltpu.VMEM((tc, 256), BF16),
            pltpu.VMEM((2, 2 * tile, tc), F32),
            pltpu.VMEM((2, tile, tc), BF16),
            pltpu.VMEM((2, tile, tc), BF16),
            pltpu.VMEM((144, tc), F32),
            pltpu.VMEM((128, tc), F32),
        ],
        name="decoder_grads",
        **params(14 * cells * padded * 128, 6 * cells * padded),
    )(counts, counts, hidden, turned, rows, wy, wd, zero, one, mixed, theta, sums, slopes)


def decoder_weight_grads(x, turned, ratio_rows, scale, drop, col, theta, genes, total):
    padded, cells = x.shape
    tile = gene_tile(padded)

    def kernel(
        x_ref, turned_ref, ratio_ref, scale_ref, drop_ref, col_ref, theta_ref,
        out_ref, gene_ref, right, mingle,
    ):
        @pl.when(pl.program_id(0) == 0)
        def _():
            for k in range(cells // 128):
                span = slice(k * 128, (k + 1) * 128)
                ratio = ratio_ref[0:1, span]
                right[span, 0:128] = jnp.transpose(turned_ref[:, span].astype(F32) * ratio).astype(BF16)
                index = lax.broadcasted_iota(jnp.int32, (128, 128), 0)
                wide = jnp.where(index == 0, jnp.broadcast_to(ratio, (128, 128)), 0.0)
                right[span, 128:256] = jnp.transpose(wide).astype(BF16)

        theta = theta_ref[...]
        row = lax.broadcasted_iota(jnp.int32, (tile, 128), 0) + pl.program_id(0) * tile
        inside = row < genes
        less = dot(x_ref[...], right[...])
        both = scale_ref[...] - less * jnp.concatenate([theta, theta], 1)
        factor = -1.0 / total
        mingle[pl.ds(0, tile, stride=2), :] = jnp.where(inside, both[:, 0:128] * factor, 0.0)
        mingle[pl.ds(1, tile, stride=2), :] = jnp.where(inside, drop_ref[:, 0:128] * factor, 0.0)
        out_ref[...] = mingle[...].astype(BF16)
        lane = lax.broadcasted_iota(jnp.int32, (tile, 128), 1)
        first = lane == 0
        slope = (LN2 * theta) * col_ref[...] - jnp.where(first, scale_ref[:, 128:256], 0.0)
        rows = [
            jnp.transpose(both[:, 128:256])[0:1],
            jnp.transpose(drop_ref[:, 128:256])[0:1],
            jnp.sum(jnp.transpose(slope), axis=0, keepdims=True),
        ]
        wide = lax.broadcasted_iota(jnp.int32, (8, tile), 1) + pl.program_id(0) * tile
        gene_ref[...] = jnp.where(wide < genes, stack_rows(rows) * factor, 0.0)

    whole = lambda j: (0, 0)
    down = lambda j: (j, 0)
    return pl.pallas_call(
        kernel,
        grid=(padded // tile,),
        in_specs=[
            pl.BlockSpec((tile, cells), down),
            pl.BlockSpec((128, cells), whole),
            pl.BlockSpec((8, cells), whole),
            pl.BlockSpec((tile, 256), down),
            pl.BlockSpec((tile, 256), down),
            pl.BlockSpec((tile, 128), down),
            pl.BlockSpec((tile, 128), down),
        ],
        out_specs=[
            pl.BlockSpec((2 * tile, 128), down),
            pl.BlockSpec((8, tile), lambda j: (0, j)),
        ],
        out_shape=[
            jax.ShapeDtypeStruct((2 * padded, 128), BF16),
            jax.ShapeDtypeStruct((8, padded), F32),
        ],
        scratch_shapes=[pltpu.VMEM((cells, 256), BF16), pltpu.VMEM((2 * tile, 128), F32)],
        name="decoder_weight_grads",
        **params(2 * cells * padded * 128, 2 * cells * padded),
    )(x, turned, ratio_rows, scale, drop, col, theta)


def unit_slope(act, gate):
    return gate * (1.0 + act * (1.0 - gate))


def decoder_upstream(back, pre, sums, norm_param, total, lanes):
    average, inv = norm_rows(sums, None, total)
    normed = (pre - as_column(average, lanes)) * as_column(inv, lanes)
    act = normed * as_column(norm_param[2:3], lanes) + as_column(norm_param[3:4], lanes)
    return back.astype(F32) * unit_slope(act, sigmoid(act)), normed, inv


def decoder_back_stats(back, pre, sums, norm_param, total):
    cells = pre.shape[1]
    block = min(cells, LANE_BLOCK)

    def kernel(back_ref, pre_ref, s_ref, norm_ref, out_ref):
        up, normed, _ = decoder_upstream(
            back_ref[...], pre_ref[...], s_ref[...], norm_ref[...], total, block
        )
        rows = stack_rows([lane_sums_row(up), lane_sums_row(up * normed)])

        @pl.when(pl.program_id(0) == 0)
        def _():
            out_ref[...] = rows

        @pl.when(pl.program_id(0) > 0)
        def _():
            out_ref[...] += rows

    whole = lambda i: (0, 0)
    return pl.pallas_call(
        kernel,
        grid=(cells // block,),
        in_specs=[
            pl.BlockSpec((128, block), lambda i: (0, i)),
            pl.BlockSpec((128, block), lambda i: (0, i)),
            pl.BlockSpec((8, 128), whole),
            pl.BlockSpec((4, 128), whole),
        ],
        out_specs=pl.BlockSpec((8, 128), whole),
        out_shape=jax.ShapeDtypeStruct((8, 128), F32),
        name="decoder_back_stats",
        **params(30 * cells * 128, 6 * cells * 128),
    )(back, pre, sums, norm_param)


def middle_backward(back, pre, sums_two, back_sums, gathered, sums_one, norm_param, head_low, head_bias, dec_low, total):
    cells = pre.shape[1]
    block = min(cells, LANE_BLOCK)

    def kernel(
        back_ref, pre_ref, s2_ref, bs_ref, g_ref, s1_ref, norm_ref, head_ref, bias_ref, dec_ref,
        up_ref, out_ref, small_ref,
    ):
        up, normed, inv = decoder_upstream(
            back_ref[...], pre_ref[...], s2_ref[...], norm_ref[...], total, block
        )
        bs = bs_ref[...] * (1.0 / total)
        inner = up - as_column(bs[0:1], block) - normed * as_column(bs[1:2], block)
        pre_grad = inner * as_column(norm_ref[2:3] * inv, block)
        noise, label = unpack_extra(g_ref[128:160, :])
        normed_one, act, gate, enc_out, mean, log_var, spread, latent = head_terms(
            g_ref[0:128, :], s1_ref[...], norm_ref, head_ref, bias_ref, noise, total, block
        )
        dec_in = decoder_input(latent, label)
        high, low = two_parts(pre_grad)
        dec_grad = dot_nt(dec_in, high) + dot_nt(dec_in, low)
        dec_top = dec_ref[0:16, :]
        latent_grad = dot(dec_top, high) + dot(dec_top, low)
        mean_part = latent_grad + mean * (1.0 / total)
        var_part = latent_grad * noise * (0.5 * spread) + (jnp.exp(log_var) - 1.0) * (0.5 / total)
        parts = jnp.concatenate([mean_part, var_part], axis=0)
        parts_high, parts_low = two_parts(parts)
        head_grad = dot_nt(parts_high, enc_out) + dot_nt(parts_low, enc_out)
        out_grad = dot_tn(head_ref[...], parts_high) + dot_tn(head_ref[...], parts_low)
        up_one = out_grad * unit_slope(act, gate)
        up_ref[...] = up_one
        rows = stack_rows([lane_sums_row(up_one), lane_sums_row(up_one * normed_one)])
        bias_grad = parts[:, 0:128]
        for k in range(1, block // 128):
            bias_grad = bias_grad + parts[:, k * 128 : (k + 1) * 128]
        bias_grad = jnp.broadcast_to(jnp.sum(bias_grad, axis=1, keepdims=True), (32, 128))

        @pl.when(pl.program_id(0) == 0)
        def _():
            out_ref[...] = rows
            small_ref[0:144, :] = dec_grad
            small_ref[144:176, :] = head_grad
            small_ref[176:208, :] = bias_grad

        @pl.when(pl.program_id(0) > 0)
        def _():
            out_ref[...] += rows
            small_ref[0:144, :] += dec_grad
            small_ref[144:176, :] += head_grad
            small_ref[176:208, :] += bias_grad

    whole = lambda i: (0, 0)
    lanes = lambda i: (0, i)
    return pl.pallas_call(
        kernel,
        grid=(cells // block,),
        in_specs=[
            pl.BlockSpec((128, block), lanes),
            pl.BlockSpec((128, block), lanes),
            pl.BlockSpec((8, 128), whole),
            pl.BlockSpec((8, 128), whole),
            pl.BlockSpec((160, block), lanes),
            pl.BlockSpec((8, 128), whole),
            pl.BlockSpec((4, 128), whole),
            pl.BlockSpec((32, 128), whole),
            pl.BlockSpec((32, 128), whole),
            pl.BlockSpec((144, 128), whole),
        ],
        out_specs=[
            pl.BlockSpec((128, block), lanes),
            pl.BlockSpec((8, 128), whole),
            pl.BlockSpec((208, 128), whole),
        ],
        out_shape=[
            jax.ShapeDtypeStruct((128, cells), F32),
            jax.ShapeDtypeStruct((8, 128), F32),
            jax.ShapeDtypeStruct((208, 128), F32),
        ],
        name="middle_backward",
        **params(2 * cells * 128 * 800, 12 * cells * 128),
    )(back, pre, sums_two, back_sums, gathered, sums_one, norm_param, head_low, head_bias, dec_low)


def encoder_weight_grads(up, gathered, sums, back_sums, norm_param, counts, total, place):
    genes, cells = counts.shape
    padded = round_up(genes, 128)
    tile = gene_tile(padded)
    half = CELL_BLOCK
    tc = 2 * half

    def kernel(up_ref, g_ref, s_ref, bs_ref, norm_ref, cnt_a, cnt_b, out_ref, acc, xs):
        average, inv = norm_rows(s_ref[...], None, total)
        normed = (g_ref[...].astype(F32) - as_column(average, tc)) * as_column(inv, tc)
        bs = bs_ref[...] * (1.0 / total)
        inner = up_ref[...] - as_column(bs[0:1], tc) - normed * as_column(bs[1:2], tc)
        grad = jnp.transpose(inner * as_column(norm_ref[0:1] * inv, tc)).astype(BF16)

        @pl.when(pl.program_id(0) == 0)
        def _():
            acc[...] = jnp.zeros(acc.shape, F32)

        for j in range(padded // tile):
            for r in range(0, tile, 16):
                at = slice(j * tile + r, j * tile + r + 16)
                xs[at, 0:half] = log_counts(cnt_a[at, :], j * tile + r, genes)[1]
                xs[at, half:tc] = log_counts(cnt_b[at, :], j * tile + r, genes)[1]
            span = slice(j * tile, (j + 1) * tile)
            acc[span, :] += dot(xs[span, :], grad)

        @pl.when(pl.program_id(0) == pl.num_programs(0) - 1)
        def _():
            out_ref[...] = acc[...].astype(BF16)

    whole = lambda i: (0, 0)
    return pl.pallas_call(
        kernel,
        grid=(cells // tc,),
        in_specs=[
            pl.BlockSpec((128, tc), lambda i: (0, i)),
            pl.BlockSpec((128, tc), lambda i: (0, i)),
            pl.BlockSpec((8, 128), whole),
            pl.BlockSpec((8, 128), whole),
            pl.BlockSpec((4, 128), whole),
            pl.BlockSpec((padded, half), lambda i: (0, place(2 * i))),
            pl.BlockSpec((padded, half), lambda i: (0, place(2 * i + 1))),
        ],
        out_specs=pl.BlockSpec((padded, 128), whole),
        out_shape=jax.ShapeDtypeStruct((padded, 128), BF16),
        scratch_shapes=[pltpu.VMEM((padded, 128), F32), pltpu.VMEM((padded, tc), BF16)],
        name="encoder_weight_grads",
        **params(2 * cells * padded * 128, 4 * cells * padded),
    )(up, gathered, sums, back_sums, norm_param, counts, counts)


def adam_update(master, first, second, grad, rate):
    first_new = BETA_ONE * first + (1.0 - BETA_ONE) * grad
    second_new = BETA_TWO * second + (1.0 - BETA_TWO) * grad * grad
    first_hat = first_new * (1.0 / (1.0 - BETA_ONE**STEP))
    second_hat = second_new * (1.0 / (1.0 - BETA_TWO**STEP))
    master_new = master - rate * (
        first_hat / (jnp.sqrt(second_hat) + ADAM_EPS) + DECAY_RATE * master
    )
    return master_new, first_new, second_new


def adam_kernel(factor, enc_grad, out_grad, gene_grad, enc, out, gene):
    genes = enc[0].shape[0]
    padded = enc_grad.shape[0]
    tile = 2 * gene_tile(padded)

    def kernel(f_ref, eg_ref, og_ref, gg_ref, *refs):
        e_in, o_in, g_in = refs[0:3], refs[3:6], refs[6:9]
        e_out, o_out, g_out = refs[9:13], refs[13:17], refs[17:20]
        factor = f_ref[0:1, 0:1]
        for grad_ref, into, out_of, rate in (
            (eg_ref, e_in, e_out, G ** (-0.5)),
            (og_ref, o_in, o_out, H ** (-0.5)),
        ):
            for r in range(0, into[0].shape[0], 64):
                at = slice(r, r + 64)
                grad = grad_ref[at, :].astype(F32) * factor
                new = adam_update(into[0][at, :], into[1][at, :], into[2][at, :], grad, rate)
                for k in range(3):
                    out_of[k][at, :] = new[k]
                out_of[3][at, :] = new[0].astype(BF16)
        grad = gg_ref[0:3, :] * factor
        new = adam_update(g_in[0][...], g_in[1][...], g_in[2][...], grad, 0.3)
        for k in range(3):
            g_out[k][...] = new[k]

    e_spec = pl.BlockSpec((tile, 128), lambda j: (j, 0))
    o_spec = pl.BlockSpec((2 * tile, 128), lambda j: (j, 0))
    g_spec = pl.BlockSpec((3, tile), lambda j: (0, j))
    shape = jax.ShapeDtypeStruct
    return pl.pallas_call(
        kernel,
        grid=(-(-padded // tile),),
        in_specs=[
            pl.BlockSpec((8, 128), lambda j: (0, 0)),
            e_spec,
            o_spec,
            pl.BlockSpec((8, tile), lambda j: (0, j)),
        ]
        + [e_spec] * 3
        + [o_spec] * 3
        + [g_spec] * 3,
        out_specs=[e_spec] * 4 + [o_spec] * 4 + [g_spec] * 3,
        out_shape=[shape((genes, 128), F32)] * 3
        + [shape((genes, 128), BF16)]
        + [shape((2 * genes, 128), F32)] * 3
        + [shape((2 * genes, 128), BF16)]
        + [shape((3, genes), F32)] * 3,
        name="adam",
        **params(100 * 384 * padded, 28 * 384 * padded),
    )(factor, enc_grad, out_grad, gene_grad, *enc, *out, *gene)


def swap(value, axis, bit):
    return lax.ppermute(value, axis, [(k, k ^ bit) for k in range(lax.axis_size(axis))])


def steps_of(axis):
    bits = []
    bit = 1
    while bit < lax.axis_size(axis):
        bits.append(bit)
        bit *= 2
    return bits


def sum_all(value, axis):
    for bit in steps_of(axis):
        value = value + swap(value, axis, bit)
    return value


def my_bit(axis, bit):
    return (lax.axis_index(axis) // bit) % 2


def scatter_sum(value, axis, dim):
    for bit in steps_of(axis):
        half = value.shape[dim] // 2
        mine = my_bit(axis, bit)
        keep = lax.dynamic_slice_in_dim(value, mine * half, half, dim)
        send = lax.dynamic_slice_in_dim(value, (1 - mine) * half, half, dim)
        value = keep.astype(F32) + swap(send.astype(BF16), axis, bit).astype(F32)
    return value


def gather_parts(value, axis, dim):
    for bit in reversed(steps_of(axis)):
        other = swap(value, axis, bit)
        mine = my_bit(axis, bit)
        low = lax.select(mine == 0, value, other)
        high = lax.select(mine == 0, other, value)
        value = lax.concatenate([low, high], dim)
    return value


def spread_all(value, axis):
    devices = lax.axis_size(axis)
    copies = jnp.broadcast_to(value[None], (devices,) + value.shape)
    return lax.all_to_all(copies, axis, 0, 0, tiled=True)


def gene_rows(value):
    return value.transpose(2, 0, 1).reshape(-1, 128)


def from_gene_rows(value):
    return value.reshape(-1, 2, 128).transpose(1, 2, 0)


def squared(value):
    value = value.astype(F32)
    return jnp.sum(value * value)


def per_device(
    counts, labels, noise_draw, enc_weight, enc_first, enc_second, out_weight, out_first, out_second,
    gene_param, gene_first, gene_second, head_weight, head_first, head_second, head_bias, bias_first,
    bias_second, dec_weight, dec_first, dec_second, norm_param, norm_first, norm_second,
):
    gene_devs = lax.axis_size("gene")
    cell_devs = lax.axis_size("cell")
    cells, genes = counts.shape
    own = noise_draw.shape[0]
    total = cells * cell_devs
    padded = round_up(genes, 128)

    head_t = head_weight.T.astype(BF16)
    gap = jnp.zeros((6, 128), BF16)
    head_low = jnp.concatenate([head_t[:L], gap, head_t[L:], gap], 0)
    bias_gap = jnp.zeros((6,), F32)
    bias_col = jnp.concatenate([head_bias[:L], bias_gap, head_bias[L:], bias_gap])
    bias_col = jnp.broadcast_to(bias_col[:, None], (32, 128))
    dec_b = dec_weight.astype(BF16)
    dec_low = jnp.concatenate([dec_b[:L], gap, dec_b[L:]], 0)

    noise_t = noise_draw.T
    noise_high, noise_rest = two_parts(noise_t)
    label_row = labels.astype(BF16)[None]
    extra_gap = jnp.zeros((5, own), BF16)
    extra = jnp.concatenate(
        [noise_high, label_row, extra_gap, noise_rest, jnp.zeros((6, own), BF16)], 0
    )

    place = lambda i: turned_block(i, gene_devs, own // CELL_BLOCK)
    counts_t = counts.T
    partial, tot_rows = encoder_sums(counts_t, enc_weight, place)
    mine = scatter_sum(partial, "gene", 1)
    gathered = gather_parts(jnp.concatenate([mine.astype(BF16), extra], 0), "gene", 1)
    weights = decoder_weights(gene_rows(out_weight), gene_param)

    sums_one = sum_all(hidden_stats(gathered), "cell")
    pre, stats_two = encoder_heads(
        gathered, sums_one, norm_param, head_low, bias_col, dec_low, total
    )
    sums_two = sum_all(stats_two, "cell")
    hidden, turned, rows = decoder_scan(
        pre, sums_two, norm_param, tot_rows, weights[0], total, gene_devs
    )
    rows = lax.all_to_all(rows, "gene", 0, 0, tiled=True)
    x_soft, back_part, mix, scale_sum, scale, drop, col, loss_rows = decoder_grads(
        counts_t, hidden, turned, rows, weights, place
    )
    cell_sum = jnp.sum(lax.all_to_all(scale_sum, "gene", 0, 0, tiled=True), 0)
    cell_total = jnp.sum(rows[:, 1], 0)[None]
    back_part = (back_part - cell_sum * mix) * (-1.0 / total)
    ratio = jnp.broadcast_to(cell_sum / cell_total, (8, cells))
    out_grad, gene_grad = decoder_weight_grads(
        x_soft, turned, ratio, scale, drop, col, weights[5], genes, total
    )
    back = gather_parts(scatter_sum(back_part, "gene", 1).astype(BF16), "gene", 1)
    back_stats = sum_all(decoder_back_stats(back, pre, sums_two, norm_param, total), "cell")
    up_one, enc_stats, small = middle_backward(
        back, pre, sums_two, back_stats, gathered, sums_one, norm_param, head_low, bias_col, dec_low,
        total,
    )
    enc_back = sum_all(enc_stats, "cell")
    enc_grad = encoder_weight_grads(
        up_one, gathered, sums_one, enc_back, norm_param, counts_t, total, place
    )

    out_mine = scatter_sum(out_grad, "cell", 0)
    enc_mine = scatter_sum(enc_grad, "cell", 0)
    gene_grad = sum_all(gene_grad, "cell")
    small = sum_all(small, "cell")
    out_all = gather_parts(out_mine.astype(BF16), "cell", 0)
    enc_all = gather_parts(enc_mine.astype(BF16), "cell", 0)

    dec_grad = jnp.concatenate([small[:L], small[16:144]], 0)
    head_grad = jnp.concatenate([small[144 : 144 + L], small[160 : 160 + L]], 0).T
    bias_grad = jnp.concatenate([small[176 : 176 + L, 0], small[192 : 192 + L, 0]])
    norm_grad = jnp.stack([enc_back[1], enc_back[0], back_stats[1], back_stats[0]])
    squares = (
        squared(enc_mine) + squared(out_mine) + squared(gene_grad) * (1.0 / cell_devs)
    )
    recon = -LN2 * jnp.sum(loss_rows)
    pair = jnp.broadcast_to(jnp.stack([squares, recon])[:, None], (2, 128))
    pair = jnp.sum(spread_all(pair, ("gene", "cell")), 0)
    loss_sum = pair[1, 0] + jnp.sum(sums_two[2])
    grad_norm = jnp.sqrt(
        pair[0, 0] + squared(head_grad) + squared(bias_grad) + squared(dec_grad) + squared(norm_grad)
    )
    factor = jnp.minimum(1.0, CLIP_NORM / (grad_norm + 1e-06))
    new = adam_kernel(
        jnp.broadcast_to(factor, (8, 128)),
        enc_all,
        out_all,
        gene_grad,
        (enc_weight, enc_first, enc_second),
        (gene_rows(out_weight), gene_rows(out_first), gene_rows(out_second)),
        (gene_param, gene_first, gene_second),
    )
    enc_new, gene_new = new[0:4], new[8:11]
    out_new = [from_gene_rows(value) for value in new[4:8]]
    head_new = adam_update(head_weight, head_first, head_second, head_grad * factor, H ** (-0.5))
    bias_new = adam_update(head_bias, bias_first, bias_second, bias_grad * factor, 0.3)
    dec_new = adam_update(dec_weight, dec_first, dec_second, dec_grad * factor, (L + NB) ** (-0.5))
    norm_new = adam_update(norm_param, norm_first, norm_second, norm_grad * factor, 0.3)
    return (
        loss_sum,
        grad_norm,
        *enc_new[0:3],
        *out_new[0:3],
        *gene_new,
        *head_new,
        *bias_new,
        *dec_new,
        *norm_new,
        enc_new[3],
        out_new[3],
        head_new[0].astype(BF16),
        dec_new[0].astype(BF16),
    )


def solution(mesh):
    rows = P("gene", None)
    columns = P(None, None, "gene")
    genes = P(None, "gene")
    in_specs = (P("cell", "gene"), P(("cell", "gene")), P(("cell", "gene"), None))
    in_specs += (rows,) * 3 + (columns,) * 3 + (genes,) * 3 + (P(),) * 12
    out_specs = (P(), P()) + (rows,) * 3 + (columns,) * 3 + (genes,) * 3 + (P(),) * 12
    out_specs += (rows, columns, P(), P())
    return jax.shard_map(
        per_device, mesh=mesh, in_specs=in_specs, out_specs=out_specs, check_vma=False
    )
```

time: 1320 us -> 353 us (0.27)
  other arithmetic: 579 us -> 24.4 us
  blocking collectives: 271 us -> 17.8 us
  waiting for transfers between devices: 260 us -> 91.8 us
  Pallas kernels: 0 us -> 149 us
  matrix products: 129 us -> 0 us
  starting transfers between devices: 5.93 us -> 49.3 us
  local copies, waits for them, and re-layouts: 43.8 us -> 8.5 us
    reduce_sum x9 -> x5, other arithmetic: 555 us -> 2.08 us  [the longest x1 1.29 us: per_device(): loss_sum = pair[1, 0] + jnp.sum(sums_two[2])]
    psum x2 -> x0, waiting for transfers between devices: 239 us -> none  [the longest x1 121 us: per_device(): lax.psum((enc_grad, out_grad, gene_grad), 'cell')]
    psum x7 -> x0, blocking collectives: 210 us -> none  [the longest x3 121 us: moments_sum(): return lax.psum((first_part, second_part), ('gene', 'cell'))]
    pallas_call x0 -> x11, Pallas kernels: none -> 149 us  [the longest x1 63.8 us: decoder_grads(): pl.pallas_call(kernel, grid=(cells // tc,), in_specs=[pl.BlockSpec((padde...]
    dot_general x14 -> x0, matrix products: 129 us -> none  [the longest x1 66.5 us: per_device(): jnp.dot(gathered, out_low[1], preferred_element_type=jnp.float32)]
    ppermute x0 -> x32, waiting for transfers between devices: none -> 88.7 us  [swap(): lax.ppermute(value, axis, [(k, k ^ bit) for k in range(lax.axis_size(axis...]
    all_gather x5 -> x0, blocking collectives: 61 us -> none  [the longest x3 27.2 us: merged_2(): everything = jax.tree.map(lambda part: lax.all_gather(part, axis), value)]
    ppermute x0 -> x32, starting transfers between devices: none -> 46.5 us  [swap(): lax.ppermute(value, axis, [(k, k ^ bit) for k in range(lax.axis_size(axis...]
  transfers between devices with their start and end apart: 4 -> 33, of which waited for: 3 -> 26; matrix products, arithmetic and copies ran while one was open for 14% -> 6% of each run, Pallas kernels for 0% -> 11%
where the time goes in v1:
time: 353 us; the launch traced here: 351 us
  Pallas kernels  149 us (42%)
  waiting for transfers between devices  91.8 us (26%)
  starting transfers between devices  49.3 us (14%)
  other arithmetic  24.4 us (7%)
  blocking collectives  17.8 us (5%)
  between operations  10.8 us (3%)
  local copies, waits for them, and re-layouts  8.5 us (2%)
    ppermute x32, waiting for transfers between devices, swap(): lax.ppermute(value, axis, [(k, k ^ bit) for k in range(lax.axis_size(axis...  88.7 us
    pallas_call x1, Pallas kernels, decoder_grads(): pl.pallas_call(kernel, grid=(cells // tc,), in_specs=[pl.BlockSpec((padde...  63.8 us
    ppermute x32, starting transfers between devices, swap(): lax.ppermute(value, axis, [(k, k ^ bit) for k in range(lax.axis_size(axis...  46.5 us
    pallas_call x1, Pallas kernels, adam_kernel(): pl.pallas_call(kernel, grid=(-(-padded // tile),), in_specs=[pl.BlockSpec...  13 us
    pallas_call x1, Pallas kernels, encoder_sums(): pl.pallas_call(kernel, grid=(cells // tc,), in_specs=[pl.BlockSpec((padde...  12.7 us
    pallas_call x1, Pallas kernels, decoder_weight_grads(): pl.pallas_call(kernel, grid=(padded // tile,), in_specs=[pl.BlockSpec((ti...  12.5 us
    pallas_call x1, Pallas kernels, encoder_weight_grads(): pl.pallas_call(kernel, grid=(cells // tc,), in_specs=[pl.BlockSpec((128,...  10.8 us
    pallas_call x1, Pallas kernels, decoder_weights(): pl.pallas_call(kernel, grid=(padded // tile,), in_specs=[pl.BlockSpec((2...  10.1 us
  transfers between devices with their start and end apart: 33, of which 26 were waited for; matrix products, arithmetic and copies ran while one was open for 6% of the time, Pallas kernels for 11%

profile of v1, /device:TPU:0, one launch (start us, length us, event | category | flops | bytes accessed | tf_op | source)
XLA Modules:
  0.0 351.1 jit_solution(6223901720774187011)
XLA Ops:
  0.7 12.7 %encoder_sums.1 = (f32[128,2048]{1,0:T(8,128)}, f32[8,2048]{1,0:T(8,128)}) custom-call(s32[2500,2048]{1,0:T(8,128)} %bitcast.41, f32[2500,128]{1,0:T(8,128)} %refs_0_.1), custom_call_target="tpu_custom_call" | custom-call | flops 1342177280 | bytes 20971520 | tf_op jit(solution)/shard_map/encoder_sums/pallas_call | solution.py:134
  17.4 2.9 collective-permute-start.1
  20.3 3.8 %collective-permute-done.1 = bf16[128,512]{1,0:T(8,128)(2,1)S(1)} collective-permute-done((bf16[128,512]{1,0:T(8,128)(2,1)S(1)}, bf16[128,512]{1,0:T(8,128)(2,1)S(1)}, u32[]{:S(2)}, u32[]{:S(2)}) %collective-permute-start.1) | collective-permute-done | bytes 131104 | tf_op jit(solution)/shard_map/ppermute | solution.py:954
  24.1 1.8 collective-permute-start.2
  26.0 2.5 collective-permute-done.2
  28.6 1.8 collective-permute-start.3
  30.4 2.6 collective-permute-done.3
  33.1 1.8 collective-permute-start.4
  35.0 3.5 collective-permute-done.4
  41.3 1.8 hidden_stats.1
  43.2 1.8 collective-permute-start.6
  47.7 2.8 collective-permute-start.7
  53.4 4.5 %encoder_heads.1 = (f32[128,2048]{1,0:T(8,128)}, f32[8,128]{1,0:T(8,128)}) custom-call(bf16[160,2048]{1,0:T(8,128)(2,1)} %pad_maximum_fusion.1.h_ref.g_ref, f32[8,128]{1,0:T(8,128)} %add.244.s_ref.s1_ref, f32[4,128]{1,0:T(4,128)} %norm_ref.9, bf16[32,128]{1,0:T(8,128)(2,1)} %pad_maximum_fusion.13.head_ref, f32[32,128]{1,0:T(8,128)} %broadcast_in_dim.32.bias_ref, ...), custom_call_target="tpu_custom_call" | custom-call | flops 94371840 | bytes 2097152 | tf_op jit(solution)/shard_map/encoder_heads/pallas_call | solution.py:352
  57.9 1.8 collective-permute-start.8
  59.8 2.0 collective-permute-done.8
  62.4 2.8 collective-permute-start.9
  65.3 10.1 %decoder_weights.1 = (bf16[2560,256]{1,0:T(8,128)(2,1)}, bf16[2560,256]{1,0:T(8,128)(2,1)}, bf16[144,2560]{1,0:T(8,128)(2,1)}, bf16[144,2560]{1,0:T(8,128)(2,1)}...) custom-call(f32[5000,128]{1,0:T(8,128)} %bitcast.46, ...), custom_call_target="tpu_custom_call" | custom-call | flops 32768000 | bytes 6553600 | tf_op jit(solution)/shard_map/decoder_weights/pallas_call | solution.py:229
  76.0 9.2 %decoder_scan.1 = (bf16[2048,128]{1,0:T(8,128)(2,1)}, bf16[128,2048]{1,0:T(8,128)(2,1)}, f32[8,2,2048]{2,1,0:T(2,128)}) custom-call(f32[128,2048]{1,0:T(8,128)} %get-tuple-element.67.pre_ref, f32[8,128]{1,0:T(8,128)} %add.246.s_ref.s2_ref, f32[4,128]{1,0:T(4,128)} %norm_ref.9, f32[8,2048]{1,0:T(8,128)} %get-tuple-element.69.tot_ref, ...), custom_call_target="tpu_custom_call" | custom-call | flops 1342177280 | bytes 1048576 | tf_op jit(solution)/shard_map/decoder_scan/pallas_call | solution.py:418
  85.2 9.5 %all_to_all.15.rows_ref = f32[8,2,2048]{2,1,0:T(2,128)} all-to-all(f32[8,2,2048]{2,1,0:T(2,128)} %get-tuple-element.73), channel_id=1, replica_groups=mesh['gene'=8,'cell'=4] {'gene'}, dimensions={0} | all-to-all | bytes 262144 | tf_op jit(solution)/shard_map/all_to_all | solution.py:1059
  94.7 63.8 %decoder_grads.1 = (bf16[2560,2048]{1,0:T(8,128)(2,1)}, f32[128,2048]{1,0:T(8,128)}, f32[128,2048]{1,0:T(8,128)}, f32[8,1,2048]{2,1,0:T(1,128)}, f32[2560,256]{1...) custom-call(s32[2500,2048]{1,0:T(8,128)} %bitcast.42, s32[2500,2048]{1,0:T(8,128)} %bitcast.43, ...), custom_call_target="tpu_custom_call" | custom-call | flops 9395240960 | bytes 31457280 | tf_op jit(solution)/shard_map/decoder_grads/pallas_call | solution.py:592
  158.5 8.3 %all_to_all.16 = f32[8,1,2048]{2,1,0:T(1,128)S(1)} all-to-all(f32[8,1,2048]{2,1,0:T(1,128)} %get-tuple-element.82), channel_id=1, replica_groups=mesh['gene'=8,'cell'=4] {'gene'}, dimensions={0} | all-to-all | bytes 131072 | tf_op jit(solution)/shard_map/all_to_all | solution.py:1063
  166.8 1.7 subtract_multiply_fusion
  170.9 5.0 %collective-permute-done.11 = bf16[128,512]{1,0:T(8,128)(2,1)S(1)} collective-permute-done((bf16[128,512]{1,0:T(8,128)(2,1)S(1)}, bf16[128,512]{1,0:T(8,128)(2,1)S(1)}, u32[]{:S(2)}, u32[]{:S(2)}) %collective-permute-start.11) | collective-permute-done | bytes 131104 | tf_op jit(solution)/shard_map/ppermute | solution.py:954
  176.6 3.7 %collective-permute-done.12 = bf16[128,256]{1,0:T(8,128)(2,1)S(1)} collective-permute-done((bf16[128,256]{1,0:T(8,128)(2,1)S(1)}, bf16[128,256]{1,0:T(8,128)(2,1)S(1)}, u32[]{:S(2)}, u32[]{:S(2)}) %collective-permute-start.12) | collective-permute-done | bytes 65568 | tf_op jit(solution)/shard_map/ppermute | solution.py:954
  182.2 2.4 collective-permute-done.13
  187.3 12.5 %decoder_weight_grads.1 = (bf16[5120,128]{1,0:T(8,128)(2,1)}, f32[8,2560]{1,0:T(8,128)}) custom-call(bf16[2560,2048]{1,0:T(8,128)(2,1)} %get-tuple-element.86.x_ref, bf16[128,2048]{1,0:T(8,128)(2,1)} %get-tuple-element.72.turned_ref, f32[8,2048]{1,0:T(8,128)} %broadcast_in_dim.33.ratio_ref, f32[2560,256]{1,0:T(8,128)} %get-tuple-element.87.scale_ref, ...), custom_call_target="tpu_custom_call" | custom-call | flops 1342177280 | bytes 10485760 | tf_op jit(solution)/shard_map/decoder_weight_grads/pallas_call | solution.py:684
  205.7 3.7 %decoder_back_stats.1 = f32[8,128]{1,0:T(8,128)} custom-call(bf16[128,2048]{1,0:T(8,128)(2,1)} %pad_maximum_fusion.4.back_ref, f32[128,2048]{1,0:T(8,128)} %get-tuple-element.67.pre_ref, f32[8,128]{1,0:T(8,128)} %add.246.s_ref.s2_ref, f32[4,128]{1,0:T(4,128)} %norm_ref.9), custom_call_target="tpu_custom_call" | custom-call | flops 7864320 | bytes 1572864 | tf_op jit(solution)/shard_map/decoder_back_stats/pallas_call | solution.py:740
  209.4 1.7 collective-permute-start.16
  211.1 8.5 %collective-permute-done.25 = f32[8,2560]{1,0:T(8,128)S(1)} collective-permute-done((f32[8,2560]{1,0:T(8,128)S(1)}, f32[8,2560]{1,0:T(8,128)S(1)}, u32[]{:S(2)}, u32[]{:S(2)}) %collective-permute-start.25) | collective-permute-done | bytes 81952 | tf_op jit(solution)/shard_map/ppermute | solution.py:954
  222.5 3.2 collective-permute-start.17
  227.8 6.5 %middle_backward.1 = (f32[128,2048]{1,0:T(8,128)}, f32[8,128]{1,0:T(8,128)}, f32[208,128]{1,0:T(8,128)}) custom-call(bf16[128,2048]{1,0:T(8,128)(2,1)} %pad_maximum_fusion.4.back_ref, f32[128,2048]{1,0:T(8,128)} %get-tuple-element.67.pre_ref, f32[8,128]{1,0:T(8,128)} %add.246.s_ref.s2_ref, f32[8,128]{1,0:T(8,128)} %add.251.bs_ref, ...), custom_call_target="tpu_custom_call" | custom-call | flops 419430400 | bytes 3145728 | tf_op jit(solution)/shard_map/middle_backward/pallas_call | solution.py:809
  234.4 2.0 collective-permute-start.18
  238.9 3.0 collective-permute-start.19
  242.7 9.7 %collective-permute-done.19 = f32[8,128]{1,0:T(8,128)S(1)} collective-permute-done((f32[8,128]{1,0:T(8,128)S(1)}, f32[8,128]{1,0:T(8,128)S(1)}, u32[]{:S(2)}, u32[]{:S(2)}) %collective-permute-start.19) | collective-permute-done | bytes 4128 | tf_op jit(solution)/shard_map/ppermute | solution.py:954
  253.1 10.8 %encoder_weight_grads.1 = bf16[2560,128]{1,0:T(8,128)(2,1)} custom-call(f32[128,2048]{1,0:T(8,128)} %get-tuple-element.84.up_ref, bf16[160,2048]{1,0:T(8,128)(2,1)} %pad_maximum_fusion.1.h_ref.g_ref, f32[8,128]{1,0:T(8,128)} %add.244.s_ref.s1_ref, f32[8,128]{1,0:T(8,128)} %add.253.bs_ref, f32[4,128]{1,0:T(4,128)} %norm_ref.9, s32[2500,2048]{1,0:T(8,128)} %bitcast.44, ...), custom_call_target="tpu_custom_call" | custom-call | flops 1342177280 | bytes 20971520 | tf_op jit(solution)/shard_map/encoder_weight_grads/pallas_call | solution.py:870
  266.4 2.9 collective-permute-start.27
  270.1 6.0 %collective-permute-done.27 = f32[208,128]{1,0:T(8,128)S(1)} collective-permute-done((f32[208,128]{1,0:T(8,128)S(1)}, f32[208,128]{1,0:T(8,128)S(1)}, u32[]{:S(2)}, u32[]{:S(2)}) %collective-permute-start.27) | collective-permute-done | bytes 106528 | tf_op jit(solution)/shard_map/ppermute | solution.py:954
  278.2 2.4 collective-permute-done.20
  281.8 12.6 %collective-permute-done.30 = bf16[1280,128]{1,0:T(8,128)(2,1)S(1)} collective-permute-done((bf16[1280,128]{1,0:T(8,128)(2,1)S(1)}, bf16[1280,128]{1,0:T(8,128)(2,1)S(1)}, u32[]{:S(2)}, u32[]{:S(2)}) %collective-permute-start.30) | collective-permute-done | bytes 327712 | tf_op jit(solution)/shard_map/ppermute | solution.py:954
  294.5 1.8 collective-permute-done.21
  299.1 2.8 all-to-all-start.2
  302.0 1.8 collective-permute-start.31
  303.8 2.4 collective-permute-start.28
  306.2 3.1 all-to-all-done.2
  314.5 7.1 %collective-permute-done.28 = bf16[640,128]{1,0:T(8,128)(2,1)S(1)} collective-permute-done((bf16[640,128]{1,0:T(8,128)(2,1)S(1)}, bf16[640,128]{1,0:T(8,128)(2,1)S(1)}, u32[]{:S(2)}, u32[]{:S(2)}) %collective-permute-start.28) | collective-permute-done | bytes 163872 | tf_op jit(solution)/shard_map/ppermute | solution.py:954
  321.7 3.7 %collective-permute-start.29 = (bf16[1280,128]{1,0:T(8,128)(2,1)S(1)}, bf16[1280,128]{1,0:T(8,128)(2,1)S(1)}, u32[]{:S(2)}, u32[]{:S(2)}) collective-permute-start(bf16[1280,128]{1,0:T(8,128)(2,1)S(1)} %pad_maximum_fusion.6), channel_id=1, source_target_pairs={{0,1},{1,0},{2,3},{3,2},{4,5},{5,4},{6,7},{7,6},{8,9},{9,8},{10,11... | collective-permute-start | bytes 983048 | tf_op jit(solution)/shard_map/ppermute | solution.py:954
  328.1 4.8 %collective-permute-done.29 = bf16[1280,128]{1,0:T(8,128)(2,1)S(1)} collective-permute-done((bf16[1280,128]{1,0:T(8,128)(2,1)S(1)}, bf16[1280,128]{1,0:T(8,128)(2,1)S(1)}, u32[]{:S(2)}, u32[]{:S(2)}) %collective-permute-start.29) | collective-permute-done | bytes 327712 | tf_op jit(solution)/shard_map/ppermute | solution.py:954
  335.9 13.0 %adam.1 = (f32[2500,128]{1,0:T(8,128)}, f32[2500,128]{1,0:T(8,128)}, f32[2500,128]{1,0:T(8,128)}, bf16[2500,128]{1,0:T(8,128)(2,1)}, f32[5000,128]{1,0:T(8,128)}...) custom-call(f32[8,128]{1,0:T(8,128)} %broadcast_in_dim.34.f_ref, ...), custom_call_target="tpu_custom_call" | custom-call | flops 98304000 | bytes 27525120 | tf_op jit(solution)/shard_map/adam/pallas_call | solution.py:930
  (166 shorter events, 49.5 us)
Async XLA Ops:
  14.5 1.7 collective-permute-start
  15.0 15.3 %copy-start.9 = (f32[128,20]{0,1:T(8,128)S(1)}, f32[128,20]{0,1:T(8,128)}, u32[]{:S(2)}) copy-start(f32[128,20]{0,1:T(8,128)} %param.36) | copy-start | bytes 30724
  15.0 15.3 %copy-start.3 = (f32[138,128]{1,0:T(8,128)S(1)}, f32[138,128]{1,0:T(8,128)}, u32[]{:S(2)}) copy-start(f32[138,128]{1,0:T(8,128)} %param.42) | copy-start | bytes 211972
  17.3 17.6 %copy-start.13 = (f32[20]{0:T(128)S(1)}, f32[20]{0:T(128)}, u32[]{:S(2)}) copy-start(f32[20]{0:T(128)} %param.39) | copy-start | bytes 244
  17.4 6.7 %collective-permute-start.1 = (bf16[128,512]{1,0:T(8,128)(2,1)S(1)}, bf16[128,512]{1,0:T(8,128)(2,1)S(1)}, u32[]{:S(2)}, u32[]{:S(2)}) collective-permute-start(bf16[128,512]{1,0:T(8,128)(2,1)S(1)} %dynamic-slice_convert_fusion.5), channel_id=1, source_target_pairs={{0,8},{4,12},{8,0},{12,4},{16,24},{20,28},{24,16},{28,20},{1,9},{5... | collective-permute-start | bytes 393224 | tf_op jit(solution)/shard_map/ppermute | solution.py:954
  24.1 4.3 %collective-permute-start.2 = (bf16[128,256]{1,0:T(8,128)(2,1)S(1)}, bf16[128,256]{1,0:T(8,128)(2,1)S(1)}, u32[]{:S(2)}, u32[]{:S(2)}) collective-permute-start(bf16[128,256]{1,0:T(8,128)(2,1)S(1)} %dynamic-slice_convert_fusion.7), channel_id=1, source_target_pairs={{0,16},{4,20},{8,24},{12,28},{16,0},{20,4},{24,8},{28,12},{1,17},{... | collective-permute-start | bytes 196616 | tf_op jit(solution)/shard_map/ppermute | solution.py:954
  28.6 4.5 %collective-permute-start.3 = (bf16[160,256]{1,0:T(8,128)(2,1)S(1)}, bf16[160,256]{1,0:T(8,128)(2,1)S(1)}, u32[]{:S(2)}, u32[]{:S(2)}) collective-permute-start(bf16[160,256]{1,0:T(8,128)(2,1)S(1)} %concatenate.51), channel_id=1, source_target_pairs={{0,16},{4,20},{8,24},{12,28},{16,0},{20,4},{24,8},{28,12},{1,17},{... | collective-permute-start | bytes 245768 | tf_op jit(solution)/shard_map/ppermute | solution.py:954
  33.1 5.4 %collective-permute-start.4 = (bf16[160,512]{1,0:T(8,128)(2,1)S(1)}, bf16[160,512]{1,0:T(8,128)(2,1)S(1)}, u32[]{:S(2)}, u32[]{:S(2)}) collective-permute-start(bf16[160,512]{1,0:T(8,128)(2,1)S(1)} %pad_maximum_fusion.8), channel_id=1, source_target_pairs={{0,8},{4,12},{8,0},{12,4},{16,24},{20,28},{24,16},{28,20},{1,9},{5... | collective-permute-start | bytes 491528 | tf_op jit(solution)/shard_map/ppermute | solution.py:954
  38.6 1.7 collective-permute-start.5
  43.2 3.8 %collective-permute-start.6 = (f32[8,128]{1,0:T(8,128)}, f32[8,128]{1,0:T(8,128)S(1)}, u32[]{:S(2)}, u32[]{:S(2)}) collective-permute-start(f32[8,128]{1,0:T(8,128)} %hidden_stats.1), channel_id=1, source_target_pairs={{0,1},{1,0},{2,3},{3,2},{4,5},{5,4},{6,7},{7,6},{8,9},{9,8},{10,11... | collective-permute-start | bytes 12296 | tf_op jit(solution)/shard_map/ppermute | solution.py:954
  47.7 4.5 %collective-permute-start.7 = (f32[8,128]{1,0:T(8,128)S(1)}, f32[8,128]{1,0:T(8,128)S(1)}, u32[]{:S(2)}, u32[]{:S(2)}) collective-permute-start(f32[8,128]{1,0:T(8,128)S(1)} %add.243), channel_id=1, source_target_pairs={{0,2},{1,3},{2,0},{3,1},{4,6},{5,7},{6,4},{7,5},{8,10},{9,11},{10,... | collective-permute-start | bytes 12296 | tf_op jit(solution)/shard_map/ppermute | solution.py:954
  57.9 3.8 %collective-permute-start.8 = (f32[8,128]{1,0:T(8,128)}, f32[8,128]{1,0:T(8,128)S(1)}, u32[]{:S(2)}, u32[]{:S(2)}) collective-permute-start(f32[8,128]{1,0:T(8,128)} %get-tuple-element.68), channel_id=1, source_target_pairs={{0,1},{1,0},{2,3},{3,2},{4,5},{5,4},{6,7},{7,6},{8,9},{9,8},{10,11... | collective-permute-start | bytes 12296 | tf_op jit(solution)/shard_map/ppermute | solution.py:954
  62.4 12.9 %collective-permute-start.9 = (f32[8,128]{1,0:T(8,128)S(1)}, f32[8,128]{1,0:T(8,128)S(1)}, u32[]{:S(2)}, u32[]{:S(2)}) collective-permute-start(f32[8,128]{1,0:T(8,128)S(1)} %add.245), channel_id=1, source_target_pairs={{0,2},{1,3},{2,0},{3,1},{4,6},{5,7},{6,4},{7,5},{8,10},{9,11},{10,... | collective-permute-start | bytes 12296 | tf_op jit(solution)/shard_map/ppermute | solution.py:954
  168.5 1.6 collective-permute-start.10
  170.2 15.2 %copy-start.14 = (f32[8,128]{1,0:T(8,128)S(1)}, f32[8,128]{1,0:T(8,128)}, u32[]{:S(2)}) copy-start(f32[8,128]{1,0:T(8,128)} %get-tuple-element.92) | copy-start | bytes 12292
  170.3 5.6 %collective-permute-start.11 = (bf16[128,512]{1,0:T(8,128)(2,1)S(1)}, bf16[128,512]{1,0:T(8,128)(2,1)S(1)}, u32[]{:S(2)}, u32[]{:S(2)}) collective-permute-start(bf16[128,512]{1,0:T(8,128)(2,1)S(1)} %dynamic-slice_convert_fusion.4), channel_id=1, source_target_pairs={{0,8},{4,12},{8,0},{12,4},{16,24},{20,28},{24,16},{28,20},{1,9},{5... | collective-permute-start | bytes 393224 | tf_op jit(solution)/shard_map/ppermute | solution.py:954
  175.9 4.3 %collective-permute-start.12 = (bf16[128,256]{1,0:T(8,128)(2,1)S(1)}, bf16[128,256]{1,0:T(8,128)(2,1)S(1)}, u32[]{:S(2)}, u32[]{:S(2)}) collective-permute-start(bf16[128,256]{1,0:T(8,128)(2,1)S(1)} %dynamic-slice_convert_fusion.6), channel_id=1, source_target_pairs={{0,16},{4,20},{8,24},{12,28},{16,0},{20,4},{24,8},{28,12},{1,17},{... | collective-permute-start | bytes 196616 | tf_op jit(solution)/shard_map/ppermute | solution.py:954
  180.3 4.3 %collective-permute-start.13 = (bf16[128,256]{1,0:T(8,128)(2,1)S(1)}, bf16[128,256]{1,0:T(8,128)(2,1)S(1)}, u32[]{:S(2)}, u32[]{:S(2)}) collective-permute-start(bf16[128,256]{1,0:T(8,128)(2,1)S(1)} %add_convert_fusion), channel_id=1, source_target_pairs={{0,16},{4,20},{8,24},{12,28},{16,0},{20,4},{24,8},{28,12},{1,17},{... | collective-permute-start | bytes 196616 | tf_op jit(solution)/shard_map/ppermute | solution.py:954
  184.7 16.8 %collective-permute-start.14 = (bf16[128,512]{1,0:T(8,128)(2,1)S(1)}, bf16[128,512]{1,0:T(8,128)(2,1)S(1)}, u32[]{:S(2)}, u32[]{:S(2)}) collective-permute-start(bf16[128,512]{1,0:T(8,128)(2,1)S(1)} %pad_maximum_fusion.9), channel_id=1, source_target_pairs={{0,8},{4,12},{8,0},{12,4},{16,24},{20,28},{24,16},{28,20},{1,9},{5... | collective-permute-start | bytes 393224 | tf_op jit(solution)/shard_map/ppermute | solution.py:954
  199.8 4.7 %collective-permute-start.24 = (f32[8,2560]{1,0:T(8,128)}, f32[8,2560]{1,0:T(8,128)S(1)}, u32[]{:S(2)}, u32[]{:S(2)}) collective-permute-start(f32[8,2560]{1,0:T(8,128)} %get-tuple-element.91), channel_id=1, source_target_pairs={{0,1},{1,0},{2,3},{3,2},{4,5},{5,4},{6,7},{7,6},{8,9},{9,8},{10,11... | collective-permute-start | bytes 245768 | tf_op jit(solution)/shard_map/ppermute | solution.py:954
  201.5 3.3 collective-permute-start.15
  202.7 22.9 %collective-permute-start.22 = (bf16[2560,128]{1,0:T(8,128)(2,1)S(1)}, bf16[2560,128]{1,0:T(8,128)(2,1)S(1)}, u32[]{:S(2)}, u32[]{:S(2)}) collective-permute-start(bf16[2560,128]{1,0:T(8,128)(2,1)S(1)} %constant_dynamic-slice_fusion), channel_id=1, source_target_pairs={{0,1},{1,0},{2,3},{3,2},{4,5},{5,4},{6,7},{7,6},{8,9},{9,8},{10,11... | collective-permute-start | bytes 1966088 | tf_op jit(solution)/shard_map/ppermute | solution.py:954
  204.5 15.2 %collective-permute-start.25 = (f32[8,2560]{1,0:T(8,128)S(1)}, f32[8,2560]{1,0:T(8,128)S(1)}, u32[]{:S(2)}, u32[]{:S(2)}) collective-permute-start(f32[8,2560]{1,0:T(8,128)S(1)} %add.269), channel_id=1, source_target_pairs={{0,2},{1,3},{2,0},{3,1},{4,6},{5,7},{6,4},{7,5},{8,10},{9,11},{10,... | collective-permute-start | bytes 245768 | tf_op jit(solution)/shard_map/ppermute | solution.py:954
  204.9 20.8 %copy-start.1 = (bf16[5120,128]{1,0:T(8,128)(2,1)S(1)}, bf16[5120,128]{1,0:T(8,128)(2,1)}, u32[]{:S(2)}) copy-start(bf16[5120,128]{1,0:T(8,128)(2,1)} %get-tuple-element.90) | copy-start | bytes 3932164
  209.4 12.3 %collective-permute-start.16 = (f32[8,128]{1,0:T(8,128)}, f32[8,128]{1,0:T(8,128)S(1)}, u32[]{:S(2)}, u32[]{:S(2)}) collective-permute-start(f32[8,128]{1,0:T(8,128)} %decoder_back_stats.1), channel_id=1, source_target_pairs={{0,1},{1,0},{2,3},{3,2},{4,5},{5,4},{6,7},{7,6},{8,9},{9,8},{10,11... | collective-permute-start | bytes 12296 | tf_op jit(solution)/shard_map/ppermute | solution.py:954
  222.5 4.8 %collective-permute-start.17 = (f32[8,128]{1,0:T(8,128)S(1)}, f32[8,128]{1,0:T(8,128)S(1)}, u32[]{:S(2)}, u32[]{:S(2)}) collective-permute-start(f32[8,128]{1,0:T(8,128)S(1)} %add.250), channel_id=1, source_target_pairs={{0,2},{1,3},{2,0},{3,1},{4,6},{5,7},{6,4},{7,5},{8,10},{9,11},{10,... | collective-permute-start | bytes 12296 | tf_op jit(solution)/shard_map/ppermute | solution.py:954
  234.4 3.9 %collective-permute-start.18 = (f32[8,128]{1,0:T(8,128)}, f32[8,128]{1,0:T(8,128)S(1)}, u32[]{:S(2)}, u32[]{:S(2)}) collective-permute-start(f32[8,128]{1,0:T(8,128)} %get-tuple-element.85), channel_id=1, source_target_pairs={{0,1},{1,0},{2,3},{3,2},{4,5},{5,4},{6,7},{7,6},{8,9},{9,8},{10,11... | collective-permute-start | bytes 12296 | tf_op jit(solution)/shard_map/ppermute | solution.py:954
  236.4 32.9 %collective-permute-start.23 = (bf16[1280,128]{1,0:T(8,128)(2,1)S(1)}, bf16[1280,128]{1,0:T(8,128)(2,1)S(1)}, u32[]{:S(2)}, u32[]{:S(2)}) collective-permute-start(bf16[1280,128]{1,0:T(8,128)(2,1)S(1)} %dynamic-slice_convert_fusion), channel_id=1, source_target_pairs={{0,2},{1,3},{2,0},{3,1},{4,6},{5,7},{6,4},{7,5},{8,10},{9,11},{10,... | collective-permute-start | bytes 983048 | tf_op jit(solution)/shard_map/ppermute | solution.py:954
  238.9 13.5 %collective-permute-start.19 = (f32[8,128]{1,0:T(8,128)S(1)}, f32[8,128]{1,0:T(8,128)S(1)}, u32[]{:S(2)}, u32[]{:S(2)}) collective-permute-start(f32[8,128]{1,0:T(8,128)S(1)} %add.252), channel_id=1, source_target_pairs={{0,2},{1,3},{2,0},{3,1},{4,6},{5,7},{6,4},{7,5},{8,10},{9,11},{10,... | collective-permute-start | bytes 12296 | tf_op jit(solution)/shard_map/ppermute | solution.py:954
  242.7 23.6 %collective-permute-start.26 = (f32[208,128]{1,0:T(8,128)}, f32[208,128]{1,0:T(8,128)S(1)}, u32[]{:S(2)}, u32[]{:S(2)}) collective-permute-start(f32[208,128]{1,0:T(8,128)} %get-tuple-element.93), channel_id=1, source_target_pairs={{0,1},{1,0},{2,3},{3,2},{4,5},{5,4},{6,7},{7,6},{8,9},{9,8},{10,11... | collective-permute-start | bytes 319496 | tf_op jit(solution)/shard_map/ppermute | solution.py:954
  263.9 16.7 %copy-start = (bf16[2560,128]{1,0:T(8,128)(2,1)S(1)}, bf16[2560,128]{1,0:T(8,128)(2,1)}, u32[]{:S(2)}) copy-start(bf16[2560,128]{1,0:T(8,128)(2,1)} %encoder_weight_grads.1) | copy-start | bytes 1966084
  265.7 14.8 %collective-permute-start.20 = (bf16[1280,128]{1,0:T(8,128)(2,1)S(1)}, bf16[1280,128]{1,0:T(8,128)(2,1)S(1)}, u32[]{:S(2)}, u32[]{:S(2)}) collective-permute-start(bf16[1280,128]{1,0:T(8,128)(2,1)S(1)} %constant_dynamic-slice_fusion.1), channel_id=1, source_target_pairs={{0,1},{1,0},{2,3},{3,2},{4,5},{5,4},{6,7},{7,6},{8,9},{9,8},{10,11... | collective-permute-start | bytes 983048 | tf_op jit(solution)/shard_map/ppermute | solution.py:954
  266.4 9.8 %collective-permute-start.27 = (f32[208,128]{1,0:T(8,128)S(1)}, f32[208,128]{1,0:T(8,128)S(1)}, u32[]{:S(2)}, u32[]{:S(2)}) collective-permute-start(f32[208,128]{1,0:T(8,128)S(1)} %add.273), channel_id=1, source_target_pairs={{0,2},{1,3},{2,0},{3,1},{4,6},{5,7},{6,4},{7,5},{8,10},{9,11},{10,... | collective-permute-start | bytes 319496 | tf_op jit(solution)/shard_map/ppermute | solution.py:954
  270.0 24.4 %collective-permute-start.30 = (bf16[1280,128]{1,0:T(8,128)(2,1)S(1)}, bf16[1280,128]{1,0:T(8,128)(2,1)S(1)}, u32[]{:S(2)}, u32[]{:S(2)}) collective-permute-start(bf16[1280,128]{1,0:T(8,128)(2,1)S(1)} %get-tuple-element.125), channel_id=1, source_target_pairs={{0,2},{1,3},{2,0},{3,1},{4,6},{5,7},{6,4},{7,5},{8,10},{9,11},{10,... | collective-permute-start | bytes 983048 | tf_op jit(solution)/shard_map/ppermute | solution.py:954
  280.7 15.6 %collective-permute-start.21 = (bf16[640,128]{1,0:T(8,128)(2,1)S(1)}, bf16[640,128]{1,0:T(8,128)(2,1)S(1)}, u32[]{:S(2)}, u32[]{:S(2)}) collective-permute-start(bf16[640,128]{1,0:T(8,128)(2,1)S(1)} %dynamic-slice_convert_fusion.3), channel_id=1, source_target_pairs={{0,2},{1,3},{2,0},{3,1},{4,6},{5,7},{6,4},{7,5},{8,10},{9,11},{10,... | collective-permute-start | bytes 491528 | tf_op jit(solution)/shard_map/ppermute | solution.py:954
  294.4 18.8 %copy-start.11 = (f32[128,20]{0,1:T(8,128)S(1)}, f32[128,20]{0,1:T(8,128)}, u32[]{:S(2)}) copy-start(f32[128,20]{0,1:T(8,128)} %param.37) | copy-start | bytes 30724
  294.4 18.8 %copy-start.12 = (f32[128,20]{0,1:T(8,128)S(1)}, f32[128,20]{0,1:T(8,128)}, u32[]{:S(2)}) copy-start(f32[128,20]{0,1:T(8,128)} %param.38) | copy-start | bytes 30724
  294.4 19.5 %copy-start.8 = (f32[4,128]{1,0:T(4,128)S(1)}, f32[4,128]{1,0:T(4,128)}, u32[]{:S(2)}) copy-start(f32[4,128]{1,0:T(4,128)} %norm_ref.9) | copy-start | bytes 6148
  294.5 19.5 %copy-start.15 = (f32[4,128]{1,0:T(4,128)S(1)}, f32[4,128]{1,0:T(4,128)}, u32[]{:S(2)}) copy-start(f32[4,128]{1,0:T(4,128)} %param.46) | copy-start | bytes 6148
  294.5 19.5 %copy-start.16 = (f32[4,128]{1,0:T(4,128)S(1)}, f32[4,128]{1,0:T(4,128)}, u32[]{:S(2)}) copy-start(f32[4,128]{1,0:T(4,128)} %param.47) | copy-start | bytes 6148
  299.1 10.3 %all-to-all-start.2 = ((f32[32,2,128]{2,1,0:T(2,128)}), f32[32,2,128]{2,1,0:T(2,128)S(1)}, u32[]{:S(2)}, u32[]{:S(2)}) async-start(f32[32,2,128]{2,1,0:T(2,128)} %broadcast_in_dim_broadcast_in_dim_broadcast_in_dim.2), calls=%async_computation.2 | async-start | bytes 65536 | tf_op jit(solution)/shard_map/all_to_all | solution.py:999
  301.9 23.5 %copy-start.17 = (f32[20]{0:T(128)S(1)}, f32[20]{0:T(128)}, u32[]{:S(2)}) copy-start(f32[20]{0:T(128)} %param.40) | copy-start | bytes 244
  301.9 23.5 %copy-start.18 = (f32[20]{0:T(128)S(1)}, f32[20]{0:T(128)}, u32[]{:S(2)}) copy-start(f32[20]{0:T(128)} %param.41) | copy-start | bytes 244
  301.9 25.4 %copy-start.6 = (f32[138,128]{1,0:T(8,128)S(1)}, f32[138,128]{1,0:T(8,128)}, u32[]{:S(2)}) copy-start(f32[138,128]{1,0:T(8,128)} %param.43) | copy-start | bytes 211972
  301.9 25.4 %copy-start.7 = (f32[138,128]{1,0:T(8,128)S(1)}, f32[138,128]{1,0:T(8,128)}, u32[]{:S(2)}) copy-start(f32[138,128]{1,0:T(8,128)} %param.44) | copy-start | bytes 211972
  302.0 31.9 %collective-permute-start.31 = (bf16[2560,128]{1,0:T(8,128)(2,1)S(1)}, bf16[2560,128]{1,0:T(8,128)(2,1)S(1)}, u32[]{:S(2)}, u32[]{:S(2)}) collective-permute-start(bf16[2560,128]{1,0:T(8,128)(2,1)S(1)} %pad_maximum_fusion.3), channel_id=1, source_target_pairs={{0,1},{1,0},{2,3},{3,2},{4,5},{5,4},{6,7},{7,6},{8,9},{9,8},{10,11... | collective-permute-start | bytes 1966088 | tf_op jit(solution)/shard_map/ppermute | solution.py:954
  303.8 17.8 %collective-permute-start.28 = (bf16[640,128]{1,0:T(8,128)(2,1)S(1)}, bf16[640,128]{1,0:T(8,128)(2,1)S(1)}, u32[]{:S(2)}, u32[]{:S(2)}) collective-permute-start(bf16[640,128]{1,0:T(8,128)(2,1)S(1)} %get-tuple-element.129), channel_id=1, source_target_pairs={{0,2},{1,3},{2,0},{3,1},{4,6},{5,7},{6,4},{7,5},{8,10},{9,11},{10,... | collective-permute-start | bytes 491528 | tf_op jit(solution)/shard_map/ppermute | solution.py:954
  321.7 11.2 %collective-permute-start.29 = (bf16[1280,128]{1,0:T(8,128)(2,1)S(1)}, bf16[1280,128]{1,0:T(8,128)(2,1)S(1)}, u32[]{:S(2)}, u32[]{:S(2)}) collective-permute-start(bf16[1280,128]{1,0:T(8,128)(2,1)S(1)} %pad_maximum_fusion.6), channel_id=1, source_target_pairs={{0,1},{1,0},{2,3},{3,2},{4,5},{5,4},{6,7},{7,6},{8,9},{9,8},{10,11... | collective-permute-start | bytes 983048 | tf_op jit(solution)/shard_map/ppermute | solution.py:954
  (5 other events, 56.0 us)
